TPU v7x, 128 devices: a whole 4x4x4 slice. The times are simulated.
128 devices in a mesh: group: 8 (over y, core), dev: 16 (over z, x).
Axes of the slice: x: 4, y: 4, z: 4, core: 2. Of those that a mesh axis runs over, the one named last changes fastest.
Arguments:
- queries: bfloat16 [3072, 1024], P(('group', 'dev')), may hold values from -12 to 12
- keys: bfloat16 [512, 256, 1024], P(('group', 'dev')), may hold values from -12 to 12
- values: bfloat16 [512, 256, 1024], P(('group', 'dev')), may hold values from -6 to 6
- frame_slot: int32 [512], replicated, may hold values from 0 to 511, each once
- covisible: int32 [12, 160], replicated, may hold values from 0 to 511, as said below
- counts: int32 [12], replicated, may hold values from 16 to 160
- out_weight: bfloat16 [1024, 1024], replicated, may hold values from -0.1875 to 0.1875
Outputs:
- projected: bfloat16 [3072, 1024], P(('group', 'dev'))
Inputs may be any that keep to these rules, and one draw needn't show every extreme that they name: `covisible`: each row lists 160 different frame numbers; query frame q attends to the first counts[q] of them. `frame_slot`: every frame is held at exactly one storage row.
All inputs are finite; a program needn't handle non-finite values.
Results may differ from a plain program's by a relative error of at most 0.02.
Values may be sent and summed in bfloat16 or wider, within the bound.
No kernel may reach another device: no remote copies, remote signals or barrier semaphores. Data moves between devices by JAX's collectives and lax.ppermute only.
A program may use at most 192 MiB of HBM per device.

v0:
```python
import functools
import itertools

import jax
import jax.numpy as jnp
from jax import lax
from jax.experimental import pallas as pl
from jax.experimental.pallas import tpu as pltpu
from jax.sharding import Mesh, PartitionSpec as P

HD = 64
LOG2E = 1.4426950408889634
TOP_STEP = 16.0
NO_TOP = -32768.0
NH = 4
WIDE = NH * HD
ALL = ("y", "core", "z", "x")
F32 = jnp.float32
BF16 = jnp.bfloat16


def spread_kernel(me, mine, theirs, out):
    first = me[1] == 0
    mine, other = mine[...].astype(F32), theirs[...].astype(F32)
    pair = jnp.concatenate([jnp.where(first, mine, other), jnp.where(first, other, mine)], axis=0).astype(BF16)
    for i in range(16):
        for c in range(2):
            out[i, c] = pair[:, c * WIDE:(c + 1) * WIDE]


def spread_rows(me, mine, theirs):
    vmem = pl.BlockSpec(memory_space=pltpu.VMEM)
    smem = pl.BlockSpec(memory_space=pltpu.SMEM)
    return pl.pallas_call(
        spread_kernel,
        out_shape=jax.ShapeDtypeStruct((16, 2, 48, WIDE), BF16),
        in_specs=[smem, vmem, vmem],
        out_specs=vmem,
        compiler_params=pltpu.CompilerParams(vmem_limit_bytes=6 * 2**20),
        name="spread",
    )(me, mine, theirs)


def attend_kernel(
    me, need, *refs, part,
):
    qs, (k0, k1, v0, _), outs = refs[:4], refs[4:8], refs[8:12]
    cnt, plan, k, vt, qm, acc, sb, top, shrink, yb, sem = refs[12:]
    my_y, my_core, my_x = me[0], me[1], me[3]
    col = pl.multiple_of(my_core * 512 + part * WIDE, WIDE)
    copies = [
        pltpu.make_async_copy(src, dst, sem.at[i])
        for i, (src, dst) in enumerate(
            [
                (k0.at[:, :, pl.ds(col, WIDE)], k.at[pl.ds(0, 4)]),
                (k1.at[:, :, pl.ds(col, WIDE)], k.at[pl.ds(4, 4)]),
                (v0.at[:, pl.ds(part * WIDE, WIDE), :], vt),
            ]
        )
    ]
    for copy in copies:
        copy.start()
    scale = HD ** -0.5 * LOG2E
    ones = jnp.ones((16, 256), BF16)

    total, slot = jnp.int32(0), jnp.int32(0)
    for qi in range(12):
        begin = total
        for j in range(8):
            plan[total] = qi + 16 * j + 256 * slot
            total = total + need[qi, j]
        cnt[qi] = total - begin
        slot = (slot + jnp.minimum(total - begin, 1)) & 3
    for u in range(8):
        plan[total + u] = 12 + 256 * slot

    def frame_of(t):
        return plan[t] & 15

    def held_of(t):
        return (plan[t] >> 4) & 7

    def slot_of(t):
        return plan[t] >> 8

    def place(r3, z, a):
        y = jnp.where(my_core == 0, a, lax.rem(my_y + 4 - r3, 4))
        x = jnp.where(my_core == 0, lax.rem(my_x + 4 - r3, 4), a)
        return [pl.multiple_of(y * 768 + (c * 16 + z * 4 + x) * 24, 8) for c in range(2)]

    spots = [[place(r3, z, a) for z in range(4) for a in range(4)] for r3 in range(4)]
    for i, spot in enumerate(spots):
        for b, rows in enumerate(spot):
            block = qs[i][b].astype(F32)
            for c, row in enumerate(rows):
                yb[pl.ds(row, 24), :WIDE] = block[c * 24:(c + 1) * 24]

    def turn(qi, _):
        rows = pl.ds(pl.multiple_of(qi * 256, 256), 256)
        zero = jnp.zeros((64, 256), BF16)
        for hp in range(NH // 2):
            turned = yb[rows, hp * 128:(hp + 1) * 128].astype(BF16).T
            qm[qi, 2 * hp] = jnp.concatenate([turned[:64], zero], axis=0)
            qm[qi, 2 * hp + 1] = jnp.concatenate([zero, turned[64:]], axis=0)
        return 0

    def turns(u, _):
        for i in range(3):
            turn(u * 3 + i, 0)
        return 0

    lax.fori_loop(0, 4, turns, 0)
    def blank(qi, _):
        @pl.when(cnt[qi] == 0)
        def _():
            rows = pl.ds(pl.multiple_of(qi * 256, 256), 256)
            yb[rows, :WIDE] = jnp.zeros((256, WIDE), F32)
            lane = lax.broadcasted_iota(jnp.int32, (256, 128), 1)
            yb[rows, WIDE:] = jnp.where(lane < NH, NO_TOP, 0.0)

        return 0

    lax.fori_loop(0, 12, blank, 0)
    for copy in copies:
        copy.wait()
    acc[...] = jnp.zeros_like(acc)
    qm[12] = jnp.zeros((NH, 128, 256), BF16)

    def score(t, p, h):
        hp = h // 2
        keys = k[held_of(t + p), :, hp * 128:(hp + 1) * 128]
        s = jnp.dot(keys, qm[frame_of(t + p), h], preferred_element_type=F32) * scale
        sb[p, h] = s
        return jnp.max(s, axis=0, keepdims=True)

    def settle(t, p, highs, old):
        first = frame_of(t + p) != frame_of(jnp.maximum(t + p - 1, 0))
        old = jnp.where(first, NO_TOP, old)
        high = jnp.concatenate(highs, axis=0)
        new = jnp.maximum(old, jnp.ceil(high * (1.0 / TOP_STEP)) * TOP_STEP)
        top[p] = new
        shrink[p] = jnp.exp2(old - new)
        return new

    def weigh(t, p, h, tops, shrinks):
        weights = jnp.exp2(sb[p, h] - tops[h:h + 1]).astype(BF16)
        vals = jnp.concatenate([vt[held_of(t + p), h * 64:(h + 1) * 64, :], ones], axis=0)
        part = jnp.dot(vals, weights, preferred_element_type=F32)
        at = slot_of(t + p)
        acc[at, h] = acc[at, h] * shrinks[h:h + 1] + part

    def finish(t, p, tops):
        qi = frame_of(t + p)

        @pl.when((qi < 12) & (frame_of(t + p + 1) != qi))
        def _():
            at = slot_of(t + p)
            rows = pl.ds(pl.multiple_of(qi * 256, 256), 256)
            totals = jnp.concatenate([acc[at, h, 64:65, :] for h in range(NH)], axis=0)
            hi = totals.astype(BF16).astype(F32)
            extra = [tops, hi, totals - hi, jnp.zeros((128 - 3 * NH, 256), F32)]
            for hp in range(NH // 2):
                both = jnp.concatenate([acc[at, 2 * hp, :64, :], acc[at, 2 * hp + 1, :64, :]], axis=0)
                yb[rows, hp * 128:(hp + 1) * 128] = both.astype(BF16).T.astype(F32)
            yb[rows, WIDE:] = jnp.concatenate(extra, axis=0).astype(BF16).T.astype(F32)

    old = jnp.full((NH, 256), NO_TOP, F32)
    for p in range(4):
        old = settle(0, p, [score(0, p, h) for h in range(NH)], old)

    def two(u, _):
        t = u * 4
        tops, shrinks = [top[p] for p in range(4)], [shrink[p] for p in range(4)]
        highs = [[] for p in range(4)]
        for p in range(4):
            for h in range(NH):
                weigh(t, p, h, tops[p], shrinks[p])
                highs[p].append(score(t + 4, p, h))
        old = tops[3]
        for p in range(4):
            old = settle(t + 4, p, highs[p], old)
        for p in range(4):
            finish(t, p, tops[p])
        return 0

    lax.fori_loop(0, (total + 3) // 4, two, 0)

    for o, spot in zip(outs, spots):
        for b, rows in enumerate(spot):
            data, tail = [], jnp.zeros((8, 128), F32)
            for c, row in enumerate(rows):
                block = yb[pl.ds(row, 24), :]
                data.append(block[:, :WIDE])
                for p in range(3):
                    piece = block[p * 8:(p + 1) * 8, WIDE:]
                    g = c * 3 + p
                    tail = tail + (pltpu.roll(piece, 16 * g, 1) if g else piece)
            data.append(jnp.concatenate([tail, jnp.zeros((8, WIDE - 128), F32)], axis=1))
            o[b] = jnp.concatenate(data, axis=0).astype(BF16)


def attend(me, need, q, k0, k1, v0, after, part):
    vmem = pl.BlockSpec(memory_space=pltpu.VMEM)
    smem = pl.BlockSpec(memory_space=pltpu.SMEM)
    whole = pl.BlockSpec(memory_space=pl.ANY)
    far = pl.BlockSpec(memory_space=pltpu.HBM)
    return pl.pallas_call(
        functools.partial(attend_kernel, part=part),
        out_shape=[jax.ShapeDtypeStruct((16, 56, WIDE), BF16)] * 4,
        in_specs=[smem] * 2 + [vmem] * 4 + [far, whole, far, whole],
        out_specs=[vmem] * 4,
        scratch_shapes=[
            pltpu.SMEM((12,), jnp.int32),
            pltpu.SMEM((112,), jnp.int32),
            pltpu.VMEM((8, 256, WIDE), BF16),
            pltpu.VMEM((8, WIDE, 256), BF16),
            pltpu.VMEM((13, NH, 128, 256), BF16),
            pltpu.VMEM((4, NH, 80, 256), F32),
            pltpu.VMEM((4, NH, 256, 256), F32),
            pltpu.VMEM((4, NH, 256), F32),
            pltpu.VMEM((4, NH, 256), F32),
            pltpu.VMEM((3072, WIDE + 128), F32),
            pltpu.SemaphoreType.DMA((3,)),
        ],
        compiler_params=pltpu.CompilerParams(vmem_limit_bytes=24 * 2**20),
        cost_estimate=pl.CostEstimate(flops=10**10, bytes_accessed=2**23, transcendentals=2 * 10**7),
        name="attend",
    )(me, need, *q, pltpu.with_memory_space_constraint(k0, pltpu.HBM), k1, pltpu.with_memory_space_constraint(v0, pltpu.HBM), after)


def turn_kernel(me, v0, v1, k, out, parts, held, turned, sem):
    parts[0] = 0
    parts[1] = 1
    col = pl.multiple_of(me[1] * 512, 512)
    copies = [
        pltpu.make_async_copy(v.at[:, :, pl.ds(col, 512)], held.at[pl.ds(i * 4, 4)], sem.at[i])
        for i, v in enumerate((v0, v1))
    ]
    for copy in copies:
        copy.start()
    backs = []
    for j in range(8):
        if j % 4 == 0:
            copies[j // 4].wait()
        for at in range(0, 512, 128):
            turned[j, at:at + 128, :] = held[j, :, at:at + 128].T
        back = pltpu.make_async_copy(turned.at[j], out.at[j], sem.at[2 + j])
        back.start()
        backs.append(back)
    for back in backs:
        back.wait()


def turn_values(me, v0, v1, k):
    smem = pl.BlockSpec(memory_space=pltpu.SMEM)
    far = pl.BlockSpec(memory_space=pltpu.HBM)
    whole = pl.BlockSpec(memory_space=pl.ANY)
    return pl.pallas_call(
        turn_kernel,
        out_shape=[pltpu.HBM((8, 512, 256), BF16), jax.ShapeDtypeStruct((2,), jnp.int32)],
        in_specs=[smem, far, whole, whole],
        out_specs=[far, smem],
        scratch_shapes=[
            pltpu.VMEM((8, 256, 512), BF16),
            pltpu.VMEM((8, 512, 256), BF16),
            pltpu.SemaphoreType.DMA((10,)),
        ],
        cost_estimate=pl.CostEstimate(flops=10**6, bytes_accessed=2**23, transcendentals=0),
        compiler_params=pltpu.CompilerParams(vmem_limit_bytes=16 * 2**20),
        name="turn",
    )(me, pltpu.with_memory_space_constraint(v0, pltpu.HBM), v1, k)


def add_up(data, tails, spread):
    n = len(data)
    best = functools.reduce(jnp.maximum, tails)
    shares = [jnp.exp2(jnp.minimum(t - best, 0.0)) for t in tails]
    total = sum(f * (pltpu.roll(t, 128 - NH, 1) + pltpu.roll(t, 128 - 2 * NH, 1)) for f, t in zip(shares, tails))
    stack = jnp.concatenate(shares, axis=0)
    groups = data[0].shape[0] // 8
    stack = jnp.concatenate([stack] + [pltpu.roll(stack, 128 - 16 * g, 1) for g in range(1, groups)], axis=0)
    wide = jnp.dot(stack.astype(BF16), spread, preferred_element_type=F32)
    numer = []
    for g in range(groups):
        at = g * 8 * n
        numer.append(
            sum(wide[at + s * 8:at + s * 8 + 8] * d[g * 8:g * 8 + 8, :].astype(F32) for s, d in enumerate(data))
        )
    return numer, best, total


def make_spread():
    src = lax.broadcasted_iota(jnp.int32, (128, WIDE), 0)
    dst = lax.broadcasted_iota(jnp.int32, (128, WIDE), 1) // HD
    return src == dst


def add_blocks(held, spread, is_top):
    data, tails = [p[:48] for p in held], [p[48:56, :128].astype(F32) for p in held]
    numer, best, total = add_up(data, tails, spread)
    total = jnp.where(is_top, total, 0.0)
    hi = total.astype(BF16).astype(F32)
    tail = jnp.where(is_top, best, 0.0) + pltpu.roll(hi, NH, 1) + pltpu.roll(total - hi, 2 * NH, 1)
    return numer, jnp.concatenate([tail, jnp.zeros((8, WIDE - 128), F32)], axis=1)


def merge_kernel(p0, p1, p2, p3, after, out):
    spread = make_spread().astype(BF16)
    is_top = lax.broadcasted_iota(jnp.int32, (8, 128), 1) % 16 < NH
    for b in range(16):
        numer, tail = add_blocks([p[b] for p in (p0, p1, p2, p3)], spread, is_top)
        out[b] = jnp.concatenate(numer + [tail], axis=0).astype(BF16)


def merge(parts, after):
    vmem = pl.BlockSpec(memory_space=pltpu.VMEM)
    return pl.pallas_call(
        merge_kernel,
        out_shape=jax.ShapeDtypeStruct((16, 56, WIDE), BF16),
        in_specs=[vmem] * 4 + [pl.BlockSpec(memory_space=pl.ANY)],
        out_specs=vmem,
        compiler_params=pltpu.CompilerParams(vmem_limit_bytes=10 * 2**20),
        name="merge",
    )(*parts, after)


def settle_rows(got):
    spread = make_spread()
    held = [got[i] for i in range(16)]
    numer, _, total = add_up([p[:48] for p in held], [p[48:56, :128].astype(F32) for p in held], spread.astype(BF16))
    totals = jnp.concatenate([total] + [pltpu.roll(total, 128 - 16 * g, 1) for g in range(1, 6)], axis=0)
    wide = jnp.dot(totals, spread.astype(F32), precision=lax.Precision.HIGHEST, preferred_element_type=F32)
    return jnp.concatenate(numer, axis=0) / wide


def first_close_kernel(got, out):
    out[...] = settle_rows(got)


def first_close(got):
    vmem = pl.BlockSpec(memory_space=pltpu.VMEM)
    return pl.pallas_call(
        first_close_kernel,
        out_shape=jax.ShapeDtypeStruct((48, WIDE), F32),
        in_specs=[vmem],
        out_specs=vmem,
        compiler_params=pltpu.CompilerParams(vmem_limit_bytes=6 * 2**20),
        name="first_close",
    )(got)


def close_kernel(me, ready, got, keep, give, both):
    both[:, :WIDE] = ready[...]
    both[:, WIDE:] = settle_rows(got)
    row = pl.multiple_of(me[1] * 24, 8)
    keep[...] = both[pl.ds(row, 24), :].astype(BF16)
    give[...] = both[pl.ds(24 - row, 24), :].astype(BF16)


def close(me, ready, got):
    vmem = pl.BlockSpec(memory_space=pltpu.VMEM)
    smem = pl.BlockSpec(memory_space=pltpu.SMEM)
    return pl.pallas_call(
        close_kernel,
        out_shape=[jax.ShapeDtypeStruct((24, 512), BF16)] * 2,
        in_specs=[smem, vmem, vmem],
        out_specs=[vmem] * 2,
        scratch_shapes=[pltpu.VMEM((48, 512), F32)],
        compiler_params=pltpu.CompilerParams(vmem_limit_bytes=6 * 2**20),
        name="close",
    )(me, ready, got)


def swap(x):
    return lax.ppermute(x, "core", [(0, 1), (1, 0)])


def shift(x, axes, by):
    pairs = []
    for y, c, z, w in itertools.product(range(4), range(2), range(4), range(4)):
        to = {"y": y, "z": z, "x": w}
        to[axes[c]] = (to[axes[c]] + by) % 4
        pairs.append((((y * 2 + c) * 4 + z) * 4 + w, ((to["y"] * 2 + c) * 4 + to["z"]) * 4 + to["x"]))
    return lax.ppermute(x, ALL, pairs)


def ring(x, axes):
    return [x] + [shift(x, axes, by) for by in (1, 2, 3)]


def spot(y, c, z, x):
    return ((y * 2 + c) * 4 + z) * 4 + x


GROUPS = [[spot(a, 0, z, w) for z in range(4) for a in range(4)] for w in range(4)] + [
    [spot(w, 1, z, a) for z in range(4) for a in range(4)] for w in range(4)
]


def exchange(x):
    return lax.all_to_all(x, ALL, 0, 0, axis_index_groups=GROUPS)


def deliver(parts, axes):
    return [parts[0]] + [shift(parts[by], axes, -by) for by in (1, 2, 3)]


def body(queries, keys, values, frame_slot, covisible, counts, out_weight):
    core = lax.axis_index("core")
    device = lax.axis_index(ALL)
    partner = device + 16 - 32 * core
    own_col = core * 512

    theirs = swap(lax.dynamic_slice_in_dim(queries, 512 - own_col, 512, 1))
    me = jnp.stack([lax.axis_index(a) for a in ALL]).astype(jnp.int32)
    mine = lax.dynamic_slice_in_dim(queries, own_col, 512, 1)
    plane = exchange(spread_rows(me, mine, theirs))
    k_theirs, v_theirs = swap(keys), swap(values)
    v_turned, parts = turn_values(me, values, v_theirs, k_theirs)
    q_parts = [ring(lax.dynamic_index_in_dim(plane, parts[c], 1, False), "xy") for c in range(2)]

    four = jnp.arange(4, dtype=jnp.int32)
    slots = jnp.concatenate([device * 4 + four, partner * 4 + four])
    frame_ids = jnp.arange(frame_slot.shape[0], dtype=jnp.int32)
    local = jnp.sum(jnp.where(frame_slot[None, :] == slots[:, None], frame_ids[None, :], 0), axis=1)
    used = jnp.arange(covisible.shape[1], dtype=jnp.int32)[None, :] < counts[:, None]
    need = jnp.any((covisible[:, None, :] == local[None, :, None]) & used[:, None, :], axis=2)
    need = need.astype(jnp.int32)

    early = attend(me, need, q_parts[0], keys, k_theirs, v_turned, q_parts[0][0], 0)
    late = attend(me, need, q_parts[1], keys, k_theirs, v_turned, early[0], 1)
    early = exchange(merge(deliver(early, "xy"), late[0]))
    late = exchange(merge(deliver(late, "xy"), late[0]))
    keep, give = close(me, first_close(early), late)
    give = swap(give)
    first = core == 0
    rows = jnp.concatenate([jnp.where(first, keep, give), jnp.where(first, give, keep)], axis=1)
    return jnp.dot(rows, out_weight, preferred_element_type=F32).astype(BF16)


def solution(mesh):
    fine = Mesh(mesh.devices.reshape(4, 2, 4, 4), ALL)
    return jax.shard_map(
        body,
        mesh=fine,
        in_specs=(P(ALL, None), P(ALL, None, None), P(ALL, None, None), P(), P(), P(), P()),
        out_specs=P(ALL, None),
        check_vma=False,
    )
```

profile of v0, /device:TPU:1, one launch (start us, length us, event | category | flops | bytes accessed | tf_op | source)
XLA Modules:
  0.0 110.5 jit_solution(8605326939589987318)
XLA Ops:
  0.0 1.4 %collective-permute-start.1 = (bf16[4,256,1024]{2,1,0:T(8,128)(2,1)}, bf16[4,256,1024]{2,1,0:T(8,128)(2,1)}, u32[]{:S(2)}, u32[]{:S(2)}) collective-permute-start(bf16[4,256,1024]{2,1,0:T(8,128)(2,1)} %v0.1), channel_id=1, source_target_pairs={{0,16},{16,0},{1,17},{17,1},{2,18},{18,2},{3,19},{19,3},{4,20},{20... | collective-permute-start | bytes 6291464 | tf_op jit(solution)/shard_map/ppermute | solution.py:375
  2.9 2.4 %collective-permute-done.theirs = bf16[24,512]{1,0:T(8,128)(2,1)S(1)} collective-permute-done((bf16[24,512]{1,0:T(8,128)(2,1)S(1)}, bf16[24,512]{1,0:T(8,128)(2,1)S(1)}, u32[]{:S(2)}, u32[]{:S(2)}) %collective-permute-start) | collective-permute-done | bytes 24608 | tf_op jit(solution)/shard_map/ppermute | solution.py:375
  5.3 1.5 %spread.1 = bf16[16,2,48,256]{3,2,1,0:T(8,128)(2,1)} custom-call(s32[4]{0:T(128)S(1)} %pad_add_fusion.me, bf16[24,512]{1,0:T(8,128)(2,1)S(1)} %get-tuple-element.34.mine, bf16[24,512]{1,0:T(8,128)(2,1)S(1)} %collective-permute-done.theirs), custom_call_target="tpu_custom_call" | custom-call | tf_op jit(solution)/shard_map/spread/pallas_call | solution.py:34
  6.8 7.7 %all-to-all-start = ((bf16[16,2,48,256]{3,2,1,0:T(8,128)(2,1)}), bf16[16,2,48,256]{3,2,1,0:T(8,128)(2,1)S(1)}, u32[]{:S(2)}, u32[]{:S(2)}) async-start(bf16[16,2,48,256]{3,2,1,0:T(8,128)(2,1)} %spread.1), calls=%async_computation | async-start | bytes 1572864 | tf_op jit(solution)/shard_map/all_to_all | solution.py:401
  14.6 3.9 %turn.1 = (bf16[8,512,256]{2,1,0:T(8,128)(2,1)}, s32[2]{0:T(128)S(1)}) custom-call(s32[4]{0:T(128)S(1)} %pad_add_fusion.me, bf16[4,256,1024]{2,1,0:T(8,128)(2,1)} %v0.1, bf16[4,256,1024]{2,1,0:T(8,128)(2,1)} %collective-permute-done.1.v1, bf16[4,256,1024]{2,1,0:T(8,128)(2,1)} %collective-permute-done.2.k.refs_5_), custom_call_target="tpu_custom_call" | custom-call | flops 1000000 | bytes 8388608 | tf_op jit(solution)/shard_map/turn/pallas_call | solution.py:258
  22.8 3.4 %all-to-all-done = bf16[16,2,48,256]{3,2,1,0:T(8,128)(2,1)S(1)} async-done(((bf16[16,2,48,256]{3,2,1,0:T(8,128)(2,1)}), bf16[16,2,48,256]{3,2,1,0:T(8,128)(2,1)S(1)}, u32[]{:S(2)}, u32[]{:S(2)}) %all-to-all-start) | async-done | bytes 786464 | tf_op jit(solution)/shard_map/all_to_all | solution.py:401
  26.3 1.6 %collective-permute-start.3 = (bf16[16,48,256]{2,1,0:T(8,128)(2,1)S(1)}, bf16[16,48,256]{2,1,0:T(8,128)(2,1)S(1)}, u32[]{:S(2)}, u32[]{:S(2)}) collective-permute-start(bf16[16,48,256]{2,1,0:T(8,128)(2,1)S(1)} %get-tuple-element.30.refs_0_.refs_7_), channel_id=1, source_target_pairs={{0,1},{1,2},{2,3},{3,0},{4,5},{5,6},{6,7},{7,4},{8,9},{9,10},{10,1... | collective-permute-start | bytes 1179656 | tf_op jit(solution)/shard_map/ppermute | solution.py:384
  27.9 2.6 %collective-permute-start.4 = (bf16[16,48,256]{2,1,0:T(8,128)(2,1)S(1)}, bf16[16,48,256]{2,1,0:T(8,128)(2,1)S(1)}, u32[]{:S(2)}, u32[]{:S(2)}) collective-permute-start(bf16[16,48,256]{2,1,0:T(8,128)(2,1)S(1)} %get-tuple-element.30.refs_0_.refs_7_), channel_id=1, source_target_pairs={{0,2},{1,3},{2,0},{3,1},{4,6},{5,7},{6,4},{7,5},{8,10},{9,11},{10,... | collective-permute-start | bytes 1179656 | tf_op jit(solution)/shard_map/ppermute | solution.py:384
  33.1 1.6 %collective-permute-done.3.refs_1_ = bf16[16,48,256]{2,1,0:T(8,128)(2,1)S(1)} collective-permute-done((bf16[16,48,256]{2,1,0:T(8,128)(2,1)S(1)}, bf16[16,48,256]{2,1,0:T(8,128)(2,1)S(1)}, u32[]{:S(2)}, u32[]{:S(2)}) %collective-permute-start.3) | collective-permute-done | bytes 393248 | tf_op jit(solution)/shard_map/ppermute | solution.py:384
  34.7 1.5 %collective-permute-start.11 = (bf16[16,48,256]{2,1,0:T(8,128)(2,1)S(1)}, bf16[16,48,256]{2,1,0:T(8,128)(2,1)S(1)}, u32[]{:S(2)}, u32[]{:S(2)}) collective-permute-start(bf16[16,48,256]{2,1,0:T(8,128)(2,1)S(1)} %get-tuple-element.29.refs_0_), channel_id=1, source_target_pairs={{0,3},{1,0},{2,1},{3,2},{4,7},{5,4},{6,5},{7,6},{8,11},{9,8},{10,9... | collective-permute-start | bytes 1179656 | tf_op jit(solution)/shard_map/ppermute | solution.py:384
  36.2 4.0 %collective-permute-done.4.refs_2_ = bf16[16,48,256]{2,1,0:T(8,128)(2,1)S(1)} collective-permute-done((bf16[16,48,256]{2,1,0:T(8,128)(2,1)S(1)}, bf16[16,48,256]{2,1,0:T(8,128)(2,1)S(1)}, u32[]{:S(2)}, u32[]{:S(2)}) %collective-permute-start.4) | collective-permute-done | bytes 393248 | tf_op jit(solution)/shard_map/ppermute | solution.py:384
  40.2 11.1 %attend.2 = (bf16[16,56,256]{2,1,0:T(8,128)(2,1)S(1)}, bf16[16,56,256]{2,1,0:T(8,128)(2,1)S(1)}, bf16[16,56,256]{2,1,0:T(8,128)(2,1)S(1)}, bf16[16,56,256]{2,1,0:T(8,128)(2,1)S(1)}) custom-call(s32[4]{0:T(128)S(1)} %pad_add_fusion.me, s32[12,8]{1,0:T(8,128)S(1)} %convert_element_type.6.need, bf16[16,48,256]{2,1,0:T(8,128)(2,1)S(1)} %get-tuple-element.30.refs_0_.refs_7_, ...), custom_call_target="tpu_custom_call" | custom-call | flops 10000000000 | bytes 8388608 | tf_op jit(solution)/shard_map/attend/pallas_call | solution.py:207
  51.3 1.7 %collective-permute-start.6 = (bf16[16,56,256]{2,1,0:T(8,128)(2,1)S(1)}, bf16[16,56,256]{2,1,0:T(8,128)(2,1)S(1)}, u32[]{:S(2)}, u32[]{:S(2)}) collective-permute-start(bf16[16,56,256]{2,1,0:T(8,128)(2,1)S(1)} %get-tuple-element.20), channel_id=1, source_target_pairs={{0,3},{1,0},{2,1},{3,2},{4,7},{5,4},{6,5},{7,6},{8,11},{9,8},{10,9... | collective-permute-start | bytes 1376264 | tf_op jit(solution)/shard_map/ppermute | solution.py:384
  53.7 12.3 %attend.3 = (bf16[16,56,256]{2,1,0:T(8,128)(2,1)S(1)}, bf16[16,56,256]{2,1,0:T(8,128)(2,1)}, bf16[16,56,256]{2,1,0:T(8,128)(2,1)}, bf16[16,56,256]{2,1,0:T(8,128)(2,1)}) custom-call(s32[4]{0:T(128)S(1)} %pad_add_fusion.me, s32[12,8]{1,0:T(8,128)S(1)} %convert_element_type.6.need, bf16[16,48,256]{2,1,0:T(8,128)(2,1)S(1)} %get-tuple-element.29.refs_0_, ...), custom_call_target="tpu_custom_call" | custom-call | flops 10000000000 | bytes 8388608 | tf_op jit(solution)/shard_map/attend/pallas_call | solution.py:207
  66.0 2.0 %collective-permute-start.12 = (bf16[16,56,256]{2,1,0:T(8,128)(2,1)}, bf16[16,56,256]{2,1,0:T(8,128)(2,1)S(1)}, u32[]{:S(2)}, u32[]{:S(2)}) collective-permute-start(bf16[16,56,256]{2,1,0:T(8,128)(2,1)} %get-tuple-element.24), channel_id=1, source_target_pairs={{0,3},{1,0},{2,1},{3,2},{4,7},{5,4},{6,5},{7,6},{8,11},{9,8},{10,9... | collective-permute-start | bytes 1376264 | tf_op jit(solution)/shard_map/ppermute | solution.py:384
  68.9 1.9 %merge.2 = bf16[16,56,256]{2,1,0:T(8,128)(2,1)} custom-call(bf16[16,56,256]{2,1,0:T(8,128)(2,1)S(1)} %get-tuple-element.19.refs_7_.p0, bf16[16,56,256]{2,1,0:T(8,128)(2,1)S(1)} %collective-permute-done.6.p1, bf16[16,56,256]{2,1,0:T(8,128)(2,1)S(1)} %collective-permute-done.7.p2, bf16[16,56,256]{2,1,0:T(8,128)(2,1)S(1)} %collective-permute-done.8.p3, ...), custom_call_target="tpu_custom_call" | custom-call | tf_op jit(solution)/shard_map/merge/pallas_call | solution.py:317
  70.7 6.8 %all-to-all-start.1 = ((bf16[16,56,256]{2,1,0:T(8,128)(2,1)}), bf16[16,56,256]{2,1,0:T(8,128)(2,1)S(1)}, u32[]{:S(2)}, u32[]{:S(2)}) async-start(bf16[16,56,256]{2,1,0:T(8,128)(2,1)} %merge.2), calls=%async_computation.1 | async-start | bytes 917504 | tf_op jit(solution)/shard_map/all_to_all | solution.py:401
  77.5 1.1 %collective-permute-done.12.p1 = bf16[16,56,256]{2,1,0:T(8,128)(2,1)S(1)} collective-permute-done((bf16[16,56,256]{2,1,0:T(8,128)(2,1)}, bf16[16,56,256]{2,1,0:T(8,128)(2,1)S(1)}, u32[]{:S(2)}, u32[]{:S(2)}) %collective-permute-start.12) | collective-permute-done | bytes 458784 | tf_op jit(solution)/shard_map/ppermute | solution.py:384
  78.6 3.7 %collective-permute-done.14.p3 = bf16[16,56,256]{2,1,0:T(8,128)(2,1)} collective-permute-done((bf16[16,56,256]{2,1,0:T(8,128)(2,1)}, bf16[16,56,256]{2,1,0:T(8,128)(2,1)}, u32[]{:S(2)}, u32[]{:S(2)}) %collective-permute-start.14) | collective-permute-done | bytes 458784 | tf_op jit(solution)/shard_map/ppermute | solution.py:384
  82.3 3.0 %merge.3 = bf16[16,56,256]{2,1,0:T(8,128)(2,1)} custom-call(bf16[16,56,256]{2,1,0:T(8,128)(2,1)S(1)} %get-tuple-element.23.after.p0, bf16[16,56,256]{2,1,0:T(8,128)(2,1)S(1)} %collective-permute-done.12.p1, bf16[16,56,256]{2,1,0:T(8,128)(2,1)} %collective-permute-done.13.p2, bf16[16,56,256]{2,1,0:T(8,128)(2,1)} %collective-permute-done.14.p3, ...), custom_call_target="tpu_custom_call" | custom-call | tf_op jit(solution)/shard_map/merge/pallas_call | solution.py:317
  85.3 3.6 %all-to-all-done.1.got = bf16[16,56,256]{2,1,0:T(8,128)(2,1)S(1)} async-done(((bf16[16,56,256]{2,1,0:T(8,128)(2,1)}), bf16[16,56,256]{2,1,0:T(8,128)(2,1)S(1)}, u32[]{:S(2)}, u32[]{:S(2)}) %all-to-all-start.1) | async-done | bytes 458784 | tf_op jit(solution)/shard_map/all_to_all | solution.py:401
  88.9 3.6 %all-to-all-start.2 = ((bf16[16,56,256]{2,1,0:T(8,128)(2,1)}), bf16[16,56,256]{2,1,0:T(8,128)(2,1)S(1)}, u32[]{:S(2)}, u32[]{:S(2)}) async-start(bf16[16,56,256]{2,1,0:T(8,128)(2,1)} %merge.3), calls=%async_computation.2 | async-start | bytes 917504 | tf_op jit(solution)/shard_map/all_to_all | solution.py:401
  92.9 8.1 %all-to-all-done.2.got = bf16[16,56,256]{2,1,0:T(8,128)(2,1)S(1)} async-done(((bf16[16,56,256]{2,1,0:T(8,128)(2,1)}), bf16[16,56,256]{2,1,0:T(8,128)(2,1)S(1)}, u32[]{:S(2)}, u32[]{:S(2)}) %all-to-all-start.2) | async-done | bytes 458784 | tf_op jit(solution)/shard_map/all_to_all | solution.py:401
  102.0 6.7 %collective-permute-start.15 = (bf16[24,512]{1,0:T(8,128)(2,1)S(1)}, bf16[24,512]{1,0:T(8,128)(2,1)S(1)}, u32[]{:S(2)}, u32[]{:S(2)}) collective-permute-start(bf16[24,512]{1,0:T(8,128)(2,1)S(1)} %get-tuple-element.28), channel_id=1, source_target_pairs={{0,16},{16,0},{1,17},{17,1},{2,18},{18,2},{3,19},{19,3},{4,20},{20... | collective-permute-start | bytes 73736 | tf_op jit(solution)/shard_map/ppermute | solution.py:375
  (42 shorter events, 9.7 us)
Async XLA Ops:
  0.0 109.5 %copy-start = (bf16[1024,1024]{1,0:T(8,128)(2,1)S(1)}, bf16[1024,1024]{1,0:T(8,128)(2,1)}, u32[]{:S(2)}) copy-start(bf16[1024,1024]{1,0:T(8,128)(2,1)} %param.13) | copy-start | bytes 6291460
  0.0 14.6 %collective-permute-start.1 = (bf16[4,256,1024]{2,1,0:T(8,128)(2,1)}, bf16[4,256,1024]{2,1,0:T(8,128)(2,1)}, u32[]{:S(2)}, u32[]{:S(2)}) collective-permute-start(bf16[4,256,1024]{2,1,0:T(8,128)(2,1)} %v0.1), channel_id=1, source_target_pairs={{0,16},{16,0},{1,17},{17,1},{2,18},{18,2},{3,19},{19,3},{4,20},{20... | collective-permute-start | bytes 6291464 | tf_op jit(solution)/shard_map/ppermute | solution.py:375
  1.4 13.2 %collective-permute-start.2 = (bf16[4,256,1024]{2,1,0:T(8,128)(2,1)}, bf16[4,256,1024]{2,1,0:T(8,128)(2,1)}, u32[]{:S(2)}, u32[]{:S(2)}) collective-permute-start(bf16[4,256,1024]{2,1,0:T(8,128)(2,1)} %refs_4_.3), channel_id=1, source_target_pairs={{0,16},{16,0},{1,17},{17,1},{2,18},{18,2},{3,19},{19,3},{4,20},{20... | collective-permute-start | bytes 6291464 | tf_op jit(solution)/shard_map/ppermute | solution.py:375
  2.2 3.1 %collective-permute-start = (bf16[24,512]{1,0:T(8,128)(2,1)S(1)}, bf16[24,512]{1,0:T(8,128)(2,1)S(1)}, u32[]{:S(2)}, u32[]{:S(2)}) collective-permute-start(bf16[24,512]{1,0:T(8,128)(2,1)S(1)} %get-tuple-element.33), channel_id=1, source_target_pairs={{0,16},{16,0},{1,17},{17,1},{2,18},{18,2},{3,19},{19,3},{4,20},{20... | collective-permute-start | bytes 73736 | tf_op jit(solution)/shard_map/ppermute | solution.py:375
  6.8 19.4 %all-to-all-start = ((bf16[16,2,48,256]{3,2,1,0:T(8,128)(2,1)}), bf16[16,2,48,256]{3,2,1,0:T(8,128)(2,1)S(1)}, u32[]{:S(2)}, u32[]{:S(2)}) async-start(bf16[16,2,48,256]{3,2,1,0:T(8,128)(2,1)} %spread.1), calls=%async_computation | async-start | bytes 1572864 | tf_op jit(solution)/shard_map/all_to_all | solution.py:401
  14.6 16.6 %copy-start.2 = (s32[512]{0:T(512)S(1)}, s32[512]{0:T(512)}, u32[]{:S(2)}) copy-start(s32[512]{0:T(512)} %param.10) | copy-start | bytes 6148
  14.6 16.8 %copy-start.3 = (s32[12]{0:T(128)S(1)}, s32[12]{0:T(128)}, u32[]{:S(2)}) copy-start(s32[12]{0:T(128)} %param.12) | copy-start | bytes 148
  14.6 16.9 %copy-start.1 = (s32[12,160]{1,0:T(8,128)S(1)}, s32[12,160]{1,0:T(8,128)}, u32[]{:S(2)}) copy-start(s32[12,160]{1,0:T(8,128)} %param.11) | copy-start | bytes 23044
  26.3 8.5 %collective-permute-start.3 = (bf16[16,48,256]{2,1,0:T(8,128)(2,1)S(1)}, bf16[16,48,256]{2,1,0:T(8,128)(2,1)S(1)}, u32[]{:S(2)}, u32[]{:S(2)}) collective-permute-start(bf16[16,48,256]{2,1,0:T(8,128)(2,1)S(1)} %get-tuple-element.30.refs_0_.refs_7_), channel_id=1, source_target_pairs={{0,1},{1,2},{2,3},{3,0},{4,5},{5,6},{6,7},{7,4},{8,9},{9,10},{10,1... | collective-permute-start | bytes 1179656 | tf_op jit(solution)/shard_map/ppermute | solution.py:384
  27.9 12.3 %collective-permute-start.4 = (bf16[16,48,256]{2,1,0:T(8,128)(2,1)S(1)}, bf16[16,48,256]{2,1,0:T(8,128)(2,1)S(1)}, u32[]{:S(2)}, u32[]{:S(2)}) collective-permute-start(bf16[16,48,256]{2,1,0:T(8,128)(2,1)S(1)} %get-tuple-element.30.refs_0_.refs_7_), channel_id=1, source_target_pairs={{0,2},{1,3},{2,0},{3,1},{4,6},{5,7},{6,4},{7,5},{8,10},{9,11},{10,... | collective-permute-start | bytes 1179656 | tf_op jit(solution)/shard_map/ppermute | solution.py:384
  30.4 9.7 %collective-permute-start.5 = (bf16[16,48,256]{2,1,0:T(8,128)(2,1)S(1)}, bf16[16,48,256]{2,1,0:T(8,128)(2,1)S(1)}, u32[]{:S(2)}, u32[]{:S(2)}) collective-permute-start(bf16[16,48,256]{2,1,0:T(8,128)(2,1)S(1)} %get-tuple-element.30.refs_0_.refs_7_), channel_id=1, source_target_pairs={{0,3},{1,0},{2,1},{3,2},{4,7},{5,4},{6,5},{7,6},{8,11},{9,8},{10,9... | collective-permute-start | bytes 1179656 | tf_op jit(solution)/shard_map/ppermute | solution.py:384
  31.9 21.2 %collective-permute-start.9 = (bf16[16,48,256]{2,1,0:T(8,128)(2,1)S(1)}, bf16[16,48,256]{2,1,0:T(8,128)(2,1)S(1)}, u32[]{:S(2)}, u32[]{:S(2)}) collective-permute-start(bf16[16,48,256]{2,1,0:T(8,128)(2,1)S(1)} %get-tuple-element.29.refs_0_), channel_id=1, source_target_pairs={{0,1},{1,2},{2,3},{3,0},{4,5},{5,6},{6,7},{7,4},{8,9},{9,10},{10,1... | collective-permute-start | bytes 1179656 | tf_op jit(solution)/shard_map/ppermute | solution.py:384
  32.6 21.1 %collective-permute-start.10 = (bf16[16,48,256]{2,1,0:T(8,128)(2,1)S(1)}, bf16[16,48,256]{2,1,0:T(8,128)(2,1)S(1)}, u32[]{:S(2)}, u32[]{:S(2)}) collective-permute-start(bf16[16,48,256]{2,1,0:T(8,128)(2,1)S(1)} %get-tuple-element.29.refs_0_), channel_id=1, source_target_pairs={{0,2},{1,3},{2,0},{3,1},{4,6},{5,7},{6,4},{7,5},{8,10},{9,11},{10,... | collective-permute-start | bytes 1179656 | tf_op jit(solution)/shard_map/ppermute | solution.py:384
  34.7 19.0 %collective-permute-start.11 = (bf16[16,48,256]{2,1,0:T(8,128)(2,1)S(1)}, bf16[16,48,256]{2,1,0:T(8,128)(2,1)S(1)}, u32[]{:S(2)}, u32[]{:S(2)}) collective-permute-start(bf16[16,48,256]{2,1,0:T(8,128)(2,1)S(1)} %get-tuple-element.29.refs_0_), channel_id=1, source_target_pairs={{0,3},{1,0},{2,1},{3,2},{4,7},{5,4},{6,5},{7,6},{8,11},{9,8},{10,9... | collective-permute-start | bytes 1179656 | tf_op jit(solution)/shard_map/ppermute | solution.py:384
  51.3 17.5 %collective-permute-start.6 = (bf16[16,56,256]{2,1,0:T(8,128)(2,1)S(1)}, bf16[16,56,256]{2,1,0:T(8,128)(2,1)S(1)}, u32[]{:S(2)}, u32[]{:S(2)}) collective-permute-start(bf16[16,56,256]{2,1,0:T(8,128)(2,1)S(1)} %get-tuple-element.20), channel_id=1, source_target_pairs={{0,3},{1,0},{2,1},{3,2},{4,7},{5,4},{6,5},{7,6},{8,11},{9,8},{10,9... | collective-permute-start | bytes 1376264 | tf_op jit(solution)/shard_map/ppermute | solution.py:384
  53.0 15.8 %collective-permute-start.7 = (bf16[16,56,256]{2,1,0:T(8,128)(2,1)S(1)}, bf16[16,56,256]{2,1,0:T(8,128)(2,1)S(1)}, u32[]{:S(2)}, u32[]{:S(2)}) collective-permute-start(bf16[16,56,256]{2,1,0:T(8,128)(2,1)S(1)} %get-tuple-element.21), channel_id=1, source_target_pairs={{0,2},{1,3},{2,0},{3,1},{4,6},{5,7},{6,4},{7,5},{8,10},{9,11},{10,... | collective-permute-start | bytes 1376264 | tf_op jit(solution)/shard_map/ppermute | solution.py:384
  53.1 15.7 %collective-permute-start.8 = (bf16[16,56,256]{2,1,0:T(8,128)(2,1)S(1)}, bf16[16,56,256]{2,1,0:T(8,128)(2,1)S(1)}, u32[]{:S(2)}, u32[]{:S(2)}) collective-permute-start(bf16[16,56,256]{2,1,0:T(8,128)(2,1)S(1)} %get-tuple-element.22), channel_id=1, source_target_pairs={{0,1},{1,2},{2,3},{3,0},{4,5},{5,6},{6,7},{7,4},{8,9},{9,10},{10,1... | collective-permute-start | bytes 1376264 | tf_op jit(solution)/shard_map/ppermute | solution.py:384
  66.0 12.7 %collective-permute-start.12 = (bf16[16,56,256]{2,1,0:T(8,128)(2,1)}, bf16[16,56,256]{2,1,0:T(8,128)(2,1)S(1)}, u32[]{:S(2)}, u32[]{:S(2)}) collective-permute-start(bf16[16,56,256]{2,1,0:T(8,128)(2,1)} %get-tuple-element.24), channel_id=1, source_target_pairs={{0,3},{1,0},{2,1},{3,2},{4,7},{5,4},{6,5},{7,6},{8,11},{9,8},{10,9... | collective-permute-start | bytes 1376264 | tf_op jit(solution)/shard_map/ppermute | solution.py:384
  67.9 10.7 %collective-permute-start.13 = (bf16[16,56,256]{2,1,0:T(8,128)(2,1)}, bf16[16,56,256]{2,1,0:T(8,128)(2,1)}, u32[]{:S(2)}, u32[]{:S(2)}) collective-permute-start(bf16[16,56,256]{2,1,0:T(8,128)(2,1)} %get-tuple-element.25), channel_id=1, source_target_pairs={{0,2},{1,3},{2,0},{3,1},{4,6},{5,7},{6,4},{7,5},{8,10},{9,11},{10,... | collective-permute-start | bytes 1376264 | tf_op jit(solution)/shard_map/ppermute | solution.py:384
  68.8 13.5 %collective-permute-start.14 = (bf16[16,56,256]{2,1,0:T(8,128)(2,1)}, bf16[16,56,256]{2,1,0:T(8,128)(2,1)}, u32[]{:S(2)}, u32[]{:S(2)}) collective-permute-start(bf16[16,56,256]{2,1,0:T(8,128)(2,1)} %get-tuple-element.26), channel_id=1, source_target_pairs={{0,1},{1,2},{2,3},{3,0},{4,5},{5,6},{6,7},{7,4},{8,9},{9,10},{10,1... | collective-permute-start | bytes 1376264 | tf_op jit(solution)/shard_map/ppermute | solution.py:384
  70.7 18.2 %all-to-all-start.1 = ((bf16[16,56,256]{2,1,0:T(8,128)(2,1)}), bf16[16,56,256]{2,1,0:T(8,128)(2,1)S(1)}, u32[]{:S(2)}, u32[]{:S(2)}) async-start(bf16[16,56,256]{2,1,0:T(8,128)(2,1)} %merge.2), calls=%async_computation.1 | async-start | bytes 917504 | tf_op jit(solution)/shard_map/all_to_all | solution.py:401
  88.9 12.1 %all-to-all-start.2 = ((bf16[16,56,256]{2,1,0:T(8,128)(2,1)}), bf16[16,56,256]{2,1,0:T(8,128)(2,1)S(1)}, u32[]{:S(2)}, u32[]{:S(2)}) async-start(bf16[16,56,256]{2,1,0:T(8,128)(2,1)} %merge.3), calls=%async_computation.2 | async-start | bytes 917504 | tf_op jit(solution)/shard_map/all_to_all | solution.py:401
  102.0 7.5 %collective-permute-start.15 = (bf16[24,512]{1,0:T(8,128)(2,1)S(1)}, bf16[24,512]{1,0:T(8,128)(2,1)S(1)}, u32[]{:S(2)}, u32[]{:S(2)}) collective-permute-start(bf16[24,512]{1,0:T(8,128)(2,1)S(1)} %get-tuple-element.28), channel_id=1, source_target_pairs={{0,16},{16,0},{1,17},{17,1},{2,18},{18,2},{3,19},{19,3},{4,20},{20... | collective-permute-start | bytes 73736 | tf_op jit(solution)/shard_map/ppermute | solution.py:375
where the time goes:
time: 111 us
  starting transfers between devices  39.6 us (36%)
  Pallas kernels  35.1 us (32%)
  waiting for transfers between devices  28.8 us (26%)
  between operations  3.79 us (3%)
  local copies, waits for them, and re-layouts  1.41 us (1%)
    pallas_call x2, Pallas kernels, attend(): pl.pallas_call(functools.partial(attend_kernel, part=part), out_shape=[ja...  23.4 us
    all_to_all x3, starting transfers between devices, exchange(): return lax.all_to_all(x, ALL, 0, 0, axis_index_groups=GROUPS)  18 us
    all_to_all x3, waiting for transfers between devices, exchange(): return lax.all_to_all(x, ALL, 0, 0, axis_index_groups=GROUPS)  15.2 us
    ppermute x12, starting transfers between devices, shift(): return lax.ppermute(x, ALL, pairs)  12.9 us
    ppermute x12, waiting for transfers between devices, shift(): return lax.ppermute(x, ALL, pairs)  10.4 us
    ppermute x4, starting transfers between devices, swap(): return lax.ppermute(x, 'core', [(0, 1), (1, 0)])  8.7 us
    pallas_call x2, Pallas kernels, merge(): pl.pallas_call(merge_kernel, out_shape=jax.ShapeDtypeStruct((16, 56, WIDE...  4.85 us
    pallas_call x1, Pallas kernels, turn_values(): pl.pallas_call(turn_kernel, out_shape=[pltpu.HBM((8, 512, 256), BF16), ja...  3.94 us
  transfers between devices with their start and end apart: 19, of which 9 were waited for; matrix products, arithmetic and copies ran while one was open for 2% of the time, Pallas kernels for 31%

commit v1 on v0

--- a/solution.py
+++ b/solution.py
@@ -324,51 +324,56 @@
     )(*parts, after)
 
 
-def settle_rows(got):
+def settle_rows(got, c):
     spread = make_spread()
-    held = [got[i] for i in range(16)]
+    held = [got[i, c] for i in range(16)]
     numer, _, total = add_up([p[:48] for p in held], [p[48:56, :128].astype(F32) for p in held], spread.astype(BF16))
     totals = jnp.concatenate([total] + [pltpu.roll(total, 128 - 16 * g, 1) for g in range(1, 6)], axis=0)
     wide = jnp.dot(totals, spread.astype(F32), precision=lax.Precision.HIGHEST, preferred_element_type=F32)
     return jnp.concatenate(numer, axis=0) / wide
 
 
-def first_close_kernel(got, out):
-    out[...] = settle_rows(got)
-
-
-def first_close(got):
+def join_kernel(p0, p1, p2, p3, ready, out):
+    spread = make_spread().astype(BF16)
+    is_top = lax.broadcasted_iota(jnp.int32, (8, 128), 1) % 16 < NH
+    for b in range(16):
+        numer, tail = add_blocks([p[b] for p in (p0, p1, p2, p3)], spread, is_top)
+        out[b, 0] = ready[b]
+        out[b, 1] = jnp.concatenate(numer + [tail], axis=0).astype(BF16)
+
+
+def join(parts, ready):
     vmem = pl.BlockSpec(memory_space=pltpu.VMEM)
     return pl.pallas_call(
-        first_close_kernel,
-        out_shape=jax.ShapeDtypeStruct((48, WIDE), F32),
-        in_specs=[vmem],
+        join_kernel,
+        out_shape=jax.ShapeDtypeStruct((16, 2, 56, WIDE), BF16),
+        in_specs=[vmem] * 5,
         out_specs=vmem,
-        compiler_params=pltpu.CompilerParams(vmem_limit_bytes=6 * 2**20),
-        name="first_close",
-    )(got)
-
-
-def close_kernel(me, ready, got, keep, give, both):
-    both[:, :WIDE] = ready[...]
-    both[:, WIDE:] = settle_rows(got)
+        compiler_params=pltpu.CompilerParams(vmem_limit_bytes=10 * 2**20),
+        name="join",
+    )(*parts, ready)
+
+
+def close_kernel(me, got, keep, give, both):
+    for c in range(2):
+        both[:, c * WIDE:(c + 1) * WIDE] = settle_rows(got, c)
     row = pl.multiple_of(me[1] * 24, 8)
     keep[...] = both[pl.ds(row, 24), :].astype(BF16)
     give[...] = both[pl.ds(24 - row, 24), :].astype(BF16)
 
 
-def close(me, ready, got):
+def close(me, got):
     vmem = pl.BlockSpec(memory_space=pltpu.VMEM)
     smem = pl.BlockSpec(memory_space=pltpu.SMEM)
     return pl.pallas_call(
         close_kernel,
         out_shape=[jax.ShapeDtypeStruct((24, 512), BF16)] * 2,
-        in_specs=[smem, vmem, vmem],
+        in_specs=[smem, vmem],
         out_specs=[vmem] * 2,
         scratch_shapes=[pltpu.VMEM((48, 512), F32)],
         compiler_params=pltpu.CompilerParams(vmem_limit_bytes=6 * 2**20),
         name="close",
-    )(me, ready, got)
+    )(me, got)
 
 
 def swap(x):
@@ -385,7 +390,8 @@
 
 
 def ring(x, axes):
-    return [x] + [shift(x, axes, by) for by in (1, 2, 3)]
+    far = shift(x, axes, 2)
+    return [x, shift(x, axes, 1), far, shift(x, axes, 3)]
 
 
 def spot(y, c, z, x):
@@ -402,7 +408,8 @@
 
 
 def deliver(parts, axes):
-    return [parts[0]] + [shift(parts[by], axes, -by) for by in (1, 2, 3)]
+    far = shift(parts[2], axes, -2)
+    return [parts[0], shift(parts[1], axes, -1), far, shift(parts[3], axes, -3)]
 
 
 def body(queries, keys, values, frame_slot, covisible, counts, out_weight):
@@ -429,9 +436,8 @@
 
     early = attend(me, need, q_parts[0], keys, k_theirs, v_turned, q_parts[0][0], 0)
     late = attend(me, need, q_parts[1], keys, k_theirs, v_turned, early[0], 1)
-    early = exchange(merge(deliver(early, "xy"), late[0]))
-    late = exchange(merge(deliver(late, "xy"), late[0]))
-    keep, give = close(me, first_close(early), late)
+    early = merge(deliver(early, "xy"), late[0])
+    keep, give = close(me, exchange(join(deliver(late, "xy"), early)))
     give = swap(give)
     first = core == 0
     rows = jnp.concatenate([jnp.where(first, keep, give), jnp.where(first, give, keep)], axis=1)

time: 111 us -> 114 us (1.027); the launches traced: 111 us -> 112 us
  blocking collectives: 0 us -> 14.7 us
  starting transfers between devices: 39.6 us -> 30.2 us
  Pallas kernels: 35.1 us -> 26.6 us
  waiting for transfers between devices: 28.8 us -> 33.1 us
    ppermute x12, waiting for transfers between devices: 10.4 us -> 26.7 us  [shift(): return lax.ppermute(x, ALL, pairs)]
    all_to_all x0 -> x1, blocking collectives: none -> 14.7 us  [exchange(): return lax.all_to_all(x, ALL, 0, 0, axis_index_groups=GROUPS)]
    all_to_all x3 -> x1, waiting for transfers between devices: 15.2 us -> 3.22 us  [exchange(): return lax.all_to_all(x, ALL, 0, 0, axis_index_groups=GROUPS)]
    all_to_all x3 -> x1, starting transfers between devices: 18 us -> 7.68 us  [exchange(): return lax.all_to_all(x, ALL, 0, 0, axis_index_groups=GROUPS)]
    pallas_call x2, Pallas kernels: 23.4 us -> 17.9 us  [attend(): pl.pallas_call(functools.partial(attend_kernel, part=part), out_shape=[ja...]
    pallas_call x2 -> x1, Pallas kernels: 4.85 us -> 1.06 us  [merge(): pl.pallas_call(merge_kernel, out_shape=jax.ShapeDtypeStruct((16, 56, WIDE...]
    ppermute x12, starting transfers between devices: 12.9 us -> 15.7 us  [shift(): return lax.ppermute(x, ALL, pairs)]
    ppermute x4, starting transfers between devices: 8.7 us -> 6.9 us  [swap(): return lax.ppermute(x, 'core', [(0, 1), (1, 0)])]
  transfers between devices with their start and end apart: 19 -> 17, of which waited for: 9 -> 10; matrix products, arithmetic and copies ran while one was open for 2% -> 2% of each run, Pallas kernels for 31% -> 22%
where the time goes in v1:
time: 114 us; the launch traced here: 112 us
  waiting for transfers between devices  33.1 us (29%)
  starting transfers between devices  30.2 us (26%)
  Pallas kernels  26.6 us (23%)
  blocking collectives  14.7 us (13%)
  between operations  3.97 us (3%)
  local copies, waits for them, and re-layouts  1.43 us (1%)
    ppermute x12, waiting for transfers between devices, shift(): return lax.ppermute(x, ALL, pairs)  26.7 us
    pallas_call x2, Pallas kernels, attend(): pl.pallas_call(functools.partial(attend_kernel, part=part), out_shape=[ja...  17.9 us
    ppermute x12, starting transfers between devices, shift(): return lax.ppermute(x, ALL, pairs)  15.7 us
    all_to_all x1, blocking collectives, exchange(): return lax.all_to_all(x, ALL, 0, 0, axis_index_groups=GROUPS)  14.7 us
    all_to_all x1, starting transfers between devices, exchange(): return lax.all_to_all(x, ALL, 0, 0, axis_index_groups=GROUPS)  7.68 us
    ppermute x4, starting transfers between devices, swap(): return lax.ppermute(x, 'core', [(0, 1), (1, 0)])  6.9 us
    pallas_call x1, Pallas kernels, turn_values(): pl.pallas_call(turn_kernel, out_shape=[pltpu.HBM((8, 512, 256), BF16), ja...  3.92 us
    ppermute x4, waiting for transfers between devices, swap(): return lax.ppermute(x, 'core', [(0, 1), (1, 0)])  3.25 us
  transfers between devices with their start and end apart: 17, of which 10 were waited for; matrix products, arithmetic and copies ran while one was open for 2% of the time, Pallas kernels for 22%

profile of v1, /device:TPU:1, one launch (start us, length us, event | category | flops | bytes accessed | tf_op | source)
XLA Modules:
  0.0 111.8 jit_solution(11182436463995000231)
XLA Ops:
  0.0 1.4 %collective-permute-start.1 = (bf16[4,256,1024]{2,1,0:T(8,128)(2,1)}, bf16[4,256,1024]{2,1,0:T(8,128)(2,1)}, u32[]{:S(2)}, u32[]{:S(2)}) collective-permute-start(bf16[4,256,1024]{2,1,0:T(8,128)(2,1)} %v0.1), channel_id=1, source_target_pairs={{0,16},{16,0},{1,17},{17,1},{2,18},{18,2},{3,19},{19,3},{4,20},{20... | collective-permute-start | bytes 6291464 | tf_op jit(solution)/shard_map/ppermute | solution.py:380
  2.9 2.4 %collective-permute-done.theirs = bf16[24,512]{1,0:T(8,128)(2,1)S(1)} collective-permute-done((bf16[24,512]{1,0:T(8,128)(2,1)S(1)}, bf16[24,512]{1,0:T(8,128)(2,1)S(1)}, u32[]{:S(2)}, u32[]{:S(2)}) %collective-permute-start) | collective-permute-done | bytes 24608 | tf_op jit(solution)/shard_map/ppermute | solution.py:380
  5.3 1.5 %spread.1 = bf16[16,2,48,256]{3,2,1,0:T(8,128)(2,1)} custom-call(s32[4]{0:T(128)S(1)} %pad_add_fusion.me, bf16[24,512]{1,0:T(8,128)(2,1)S(1)} %get-tuple-element.34.mine, bf16[24,512]{1,0:T(8,128)(2,1)S(1)} %collective-permute-done.theirs), custom_call_target="tpu_custom_call" | custom-call | tf_op jit(solution)/shard_map/spread/pallas_call | solution.py:34
  6.8 7.7 %all-to-all-start = ((bf16[16,2,48,256]{3,2,1,0:T(8,128)(2,1)}), bf16[16,2,48,256]{3,2,1,0:T(8,128)(2,1)S(1)}, u32[]{:S(2)}, u32[]{:S(2)}) async-start(bf16[16,2,48,256]{3,2,1,0:T(8,128)(2,1)} %spread.1), calls=%async_computation | async-start | bytes 1572864 | tf_op jit(solution)/shard_map/all_to_all | solution.py:407
  14.6 3.9 %turn.1 = (bf16[8,512,256]{2,1,0:T(8,128)(2,1)}, s32[2]{0:T(128)S(1)}) custom-call(s32[4]{0:T(128)S(1)} %pad_add_fusion.me, bf16[4,256,1024]{2,1,0:T(8,128)(2,1)} %v0.1, bf16[4,256,1024]{2,1,0:T(8,128)(2,1)} %collective-permute-done.1.v1, bf16[4,256,1024]{2,1,0:T(8,128)(2,1)} %collective-permute-done.2.k.refs_5_), custom_call_target="tpu_custom_call" | custom-call | flops 1000000 | bytes 8388608 | tf_op jit(solution)/shard_map/turn/pallas_call | solution.py:258
  23.0 3.2 %all-to-all-done = bf16[16,2,48,256]{3,2,1,0:T(8,128)(2,1)S(1)} async-done(((bf16[16,2,48,256]{3,2,1,0:T(8,128)(2,1)}), bf16[16,2,48,256]{3,2,1,0:T(8,128)(2,1)S(1)}, u32[]{:S(2)}, u32[]{:S(2)}) %all-to-all-start) | async-done | bytes 786464 | tf_op jit(solution)/shard_map/all_to_all | solution.py:407
  26.3 3.0 %collective-permute-start.8 = (bf16[16,48,256]{2,1,0:T(8,128)(2,1)S(1)}, bf16[16,48,256]{2,1,0:T(8,128)(2,1)S(1)}, u32[]{:S(2)}, u32[]{:S(2)}) collective-permute-start(bf16[16,48,256]{2,1,0:T(8,128)(2,1)S(1)} %get-tuple-element.29.refs_0_.refs_7_), channel_id=1, source_target_pairs={{0,3},{1,0},{2,1},{3,2},{4,7},{5,4},{6,5},{7,6},{8,11},{9,8},{10,9... | collective-permute-start | bytes 1179656 | tf_op jit(solution)/shard_map/ppermute | solution.py:389
  30.7 2.4 %collective-permute-start.5 = (bf16[16,48,256]{2,1,0:T(8,128)(2,1)S(1)}, bf16[16,48,256]{2,1,0:T(8,128)(2,1)S(1)}, u32[]{:S(2)}, u32[]{:S(2)}) collective-permute-start(bf16[16,48,256]{2,1,0:T(8,128)(2,1)S(1)} %get-tuple-element.30.refs_0_), channel_id=1, source_target_pairs={{0,3},{1,0},{2,1},{3,2},{4,7},{5,4},{6,5},{7,6},{8,11},{9,8},{10,9... | collective-permute-start | bytes 1179656 | tf_op jit(solution)/shard_map/ppermute | solution.py:389
  33.1 1.3 %collective-permute-start.4 = (bf16[16,48,256]{2,1,0:T(8,128)(2,1)S(1)}, bf16[16,48,256]{2,1,0:T(8,128)(2,1)S(1)}, u32[]{:S(2)}, u32[]{:S(2)}) collective-permute-start(bf16[16,48,256]{2,1,0:T(8,128)(2,1)S(1)} %get-tuple-element.30.refs_0_), channel_id=1, source_target_pairs={{0,2},{1,3},{2,0},{3,1},{4,6},{5,7},{6,4},{7,5},{8,10},{9,11},{10,... | collective-permute-start | bytes 1179656 | tf_op jit(solution)/shard_map/ppermute | solution.py:389
  34.4 3.8 %collective-permute-done.8.refs_3_ = bf16[16,48,256]{2,1,0:T(8,128)(2,1)S(1)} collective-permute-done((bf16[16,48,256]{2,1,0:T(8,128)(2,1)S(1)}, bf16[16,48,256]{2,1,0:T(8,128)(2,1)S(1)}, u32[]{:S(2)}, u32[]{:S(2)}) %collective-permute-start.8) | collective-permute-done | bytes 393248 | tf_op jit(solution)/shard_map/ppermute | solution.py:389
  38.2 3.7 %collective-permute-done.6.refs_1_ = bf16[16,48,256]{2,1,0:T(8,128)(2,1)S(1)} collective-permute-done((bf16[16,48,256]{2,1,0:T(8,128)(2,1)S(1)}, bf16[16,48,256]{2,1,0:T(8,128)(2,1)S(1)}, u32[]{:S(2)}, u32[]{:S(2)}) %collective-permute-start.6) | collective-permute-done | bytes 393248 | tf_op jit(solution)/shard_map/ppermute | solution.py:389
  41.9 8.9 %attend.2 = (bf16[16,56,256]{2,1,0:T(8,128)(2,1)S(1)}, bf16[16,56,256]{2,1,0:T(8,128)(2,1)S(1)}, bf16[16,56,256]{2,1,0:T(8,128)(2,1)S(1)}, bf16[16,56,256]{2,1,0:T(8,128)(2,1)S(1)}) custom-call(s32[4]{0:T(128)S(1)} %pad_add_fusion.me, s32[12,8]{1,0:T(8,128)S(1)} %convert_element_type.6.need, bf16[16,48,256]{2,1,0:T(8,128)(2,1)S(1)} %get-tuple-element.29.refs_0_.refs_7_, ...), custom_call_target="tpu_custom_call" | custom-call | flops 10000000000 | bytes 8388608 | tf_op jit(solution)/shard_map/attend/pallas_call | solution.py:207
  50.9 2.5 %collective-permute-start.12 = (bf16[16,56,256]{2,1,0:T(8,128)(2,1)S(1)}, bf16[16,56,256]{2,1,0:T(8,128)(2,1)S(1)}, u32[]{:S(2)}, u32[]{:S(2)}) collective-permute-start(bf16[16,56,256]{2,1,0:T(8,128)(2,1)S(1)} %get-tuple-element.24), channel_id=1, source_target_pairs={{0,3},{1,0},{2,1},{3,2},{4,7},{5,4},{6,5},{7,6},{8,11},{9,8},{10,9... | collective-permute-start | bytes 1376264 | tf_op jit(solution)/shard_map/ppermute | solution.py:389
  53.4 8.9 %attend.3 = (bf16[16,56,256]{2,1,0:T(8,128)(2,1)S(1)}, bf16[16,56,256]{2,1,0:T(8,128)(2,1)S(1)}, bf16[16,56,256]{2,1,0:T(8,128)(2,1)S(1)}, bf16[16,56,256]{2,1,0:T(8,128)(2,1)S(1)}) custom-call(s32[4]{0:T(128)S(1)} %pad_add_fusion.me, s32[12,8]{1,0:T(8,128)S(1)} %convert_element_type.6.need, bf16[16,48,256]{2,1,0:T(8,128)(2,1)S(1)} %get-tuple-element.30.refs_0_, ...), custom_call_target="tpu_custom_call" | custom-call | flops 10000000000 | bytes 8388608 | tf_op jit(solution)/shard_map/attend/pallas_call | solution.py:207
  62.3 2.4 %collective-permute-start.9 = (bf16[16,56,256]{2,1,0:T(8,128)(2,1)S(1)}, bf16[16,56,256]{2,1,0:T(8,128)(2,1)S(1)}, u32[]{:S(2)}, u32[]{:S(2)}) collective-permute-start(bf16[16,56,256]{2,1,0:T(8,128)(2,1)S(1)} %get-tuple-element.21), channel_id=1, source_target_pairs={{0,3},{1,0},{2,1},{3,2},{4,7},{5,4},{6,5},{7,6},{8,11},{9,8},{10,9... | collective-permute-start | bytes 1376264 | tf_op jit(solution)/shard_map/ppermute | solution.py:389
  65.4 2.3 %collective-permute-start.10 = (bf16[16,56,256]{2,1,0:T(8,128)(2,1)S(1)}, bf16[16,56,256]{2,1,0:T(8,128)(2,1)S(1)}, u32[]{:S(2)}, u32[]{:S(2)}) collective-permute-start(bf16[16,56,256]{2,1,0:T(8,128)(2,1)S(1)} %get-tuple-element.22), channel_id=1, source_target_pairs={{0,2},{1,3},{2,0},{3,1},{4,6},{5,7},{6,4},{7,5},{8,10},{9,11},{10,... | collective-permute-start | bytes 1376264 | tf_op jit(solution)/shard_map/ppermute | solution.py:389
  67.9 5.7 %collective-permute-done.13.p2 = bf16[16,56,256]{2,1,0:T(8,128)(2,1)S(1)} collective-permute-done((bf16[16,56,256]{2,1,0:T(8,128)(2,1)S(1)}, bf16[16,56,256]{2,1,0:T(8,128)(2,1)S(1)}, u32[]{:S(2)}, u32[]{:S(2)}) %collective-permute-start.13) | collective-permute-done | bytes 458784 | tf_op jit(solution)/shard_map/ppermute | solution.py:389
  73.6 4.8 %collective-permute-done.14.p3 = bf16[16,56,256]{2,1,0:T(8,128)(2,1)S(1)} collective-permute-done((bf16[16,56,256]{2,1,0:T(8,128)(2,1)S(1)}, bf16[16,56,256]{2,1,0:T(8,128)(2,1)S(1)}, u32[]{:S(2)}, u32[]{:S(2)}) %collective-permute-start.14) | collective-permute-done | bytes 458784 | tf_op jit(solution)/shard_map/ppermute | solution.py:389
  78.4 1.1 merge.1.ready
  79.9 3.6 %collective-permute-done.10.p2 = bf16[16,56,256]{2,1,0:T(8,128)(2,1)S(1)} collective-permute-done((bf16[16,56,256]{2,1,0:T(8,128)(2,1)S(1)}, bf16[16,56,256]{2,1,0:T(8,128)(2,1)S(1)}, u32[]{:S(2)}, u32[]{:S(2)}) %collective-permute-start.10) | collective-permute-done | bytes 458784 | tf_op jit(solution)/shard_map/ppermute | solution.py:389
  83.5 4.7 %collective-permute-done.11.p3 = bf16[16,56,256]{2,1,0:T(8,128)(2,1)S(1)} collective-permute-done((bf16[16,56,256]{2,1,0:T(8,128)(2,1)S(1)}, bf16[16,56,256]{2,1,0:T(8,128)(2,1)S(1)}, u32[]{:S(2)}, u32[]{:S(2)}) %collective-permute-start.11) | collective-permute-done | bytes 458784 | tf_op jit(solution)/shard_map/ppermute | solution.py:389
  89.3 14.7 %all_to_all.10.got = bf16[16,2,56,256]{3,2,1,0:T(8,128)(2,1)S(1)} all-to-all(bf16[16,2,56,256]{3,2,1,0:T(8,128)(2,1)S(1)} %join.1), channel_id=1, replica_groups={{0,32,64,96,4,36,68,100,8,40,72,104,12,44,76,108},{1,33,65,97,5,37,69,1..., dimensions={0} | all-to-all | bytes 1835008 | tf_op jit(solution)/shard_map/all_to_all | solution.py:407
  104.0 1.1 %close.1 = (bf16[24,512]{1,0:T(8,128)(2,1)S(1)}, bf16[24,512]{1,0:T(8,128)(2,1)S(1)}) custom-call(s32[4]{0:T(128)S(1)} %pad_add_fusion.me, bf16[16,2,56,256]{3,2,1,0:T(8,128)(2,1)S(1)} %all_to_all.10.got), custom_call_target="tpu_custom_call" | custom-call | tf_op jit(solution)/shard_map/close/pallas_call | solution.py:368
  105.1 4.8 %collective-permute-start.15 = (bf16[24,512]{1,0:T(8,128)(2,1)S(1)}, bf16[24,512]{1,0:T(8,128)(2,1)S(1)}, u32[]{:S(2)}, u32[]{:S(2)}) collective-permute-start(bf16[24,512]{1,0:T(8,128)(2,1)S(1)} %get-tuple-element.28), channel_id=1, source_target_pairs={{0,16},{16,0},{1,17},{17,1},{2,18},{18,2},{3,19},{19,3},{4,20},{20... | collective-permute-start | bytes 73736 | tf_op jit(solution)/shard_map/ppermute | solution.py:380
  (38 shorter events, 7.9 us)
Async XLA Ops:
  0.0 110.8 %copy-start = (bf16[1024,1024]{1,0:T(8,128)(2,1)S(1)}, bf16[1024,1024]{1,0:T(8,128)(2,1)}, u32[]{:S(2)}) copy-start(bf16[1024,1024]{1,0:T(8,128)(2,1)} %param.13) | copy-start | bytes 6291460
  0.0 14.6 %collective-permute-start.1 = (bf16[4,256,1024]{2,1,0:T(8,128)(2,1)}, bf16[4,256,1024]{2,1,0:T(8,128)(2,1)}, u32[]{:S(2)}, u32[]{:S(2)}) collective-permute-start(bf16[4,256,1024]{2,1,0:T(8,128)(2,1)} %v0.1), channel_id=1, source_target_pairs={{0,16},{16,0},{1,17},{17,1},{2,18},{18,2},{3,19},{19,3},{4,20},{20... | collective-permute-start | bytes 6291464 | tf_op jit(solution)/shard_map/ppermute | solution.py:380
  1.4 13.2 %collective-permute-start.2 = (bf16[4,256,1024]{2,1,0:T(8,128)(2,1)}, bf16[4,256,1024]{2,1,0:T(8,128)(2,1)}, u32[]{:S(2)}, u32[]{:S(2)}) collective-permute-start(bf16[4,256,1024]{2,1,0:T(8,128)(2,1)} %refs_4_.3), channel_id=1, source_target_pairs={{0,16},{16,0},{1,17},{17,1},{2,18},{18,2},{3,19},{19,3},{4,20},{20... | collective-permute-start | bytes 6291464 | tf_op jit(solution)/shard_map/ppermute | solution.py:380
  2.2 3.1 %collective-permute-start = (bf16[24,512]{1,0:T(8,128)(2,1)S(1)}, bf16[24,512]{1,0:T(8,128)(2,1)S(1)}, u32[]{:S(2)}, u32[]{:S(2)}) collective-permute-start(bf16[24,512]{1,0:T(8,128)(2,1)S(1)} %get-tuple-element.33), channel_id=1, source_target_pairs={{0,16},{16,0},{1,17},{17,1},{2,18},{18,2},{3,19},{19,3},{4,20},{20... | collective-permute-start | bytes 73736 | tf_op jit(solution)/shard_map/ppermute | solution.py:380
  6.8 19.4 %all-to-all-start = ((bf16[16,2,48,256]{3,2,1,0:T(8,128)(2,1)}), bf16[16,2,48,256]{3,2,1,0:T(8,128)(2,1)S(1)}, u32[]{:S(2)}, u32[]{:S(2)}) async-start(bf16[16,2,48,256]{3,2,1,0:T(8,128)(2,1)} %spread.1), calls=%async_computation | async-start | bytes 1572864 | tf_op jit(solution)/shard_map/all_to_all | solution.py:407
  14.6 15.4 %copy-start.2 = (s32[512]{0:T(512)S(1)}, s32[512]{0:T(512)}, u32[]{:S(2)}) copy-start(s32[512]{0:T(512)} %param.10) | copy-start | bytes 6148
  14.6 15.6 %copy-start.3 = (s32[12]{0:T(128)S(1)}, s32[12]{0:T(128)}, u32[]{:S(2)}) copy-start(s32[12]{0:T(128)} %param.12) | copy-start | bytes 148
  14.6 15.7 %copy-start.1 = (s32[12,160]{1,0:T(8,128)S(1)}, s32[12,160]{1,0:T(8,128)}, u32[]{:S(2)}) copy-start(s32[12,160]{1,0:T(8,128)} %param.11) | copy-start | bytes 23044
  26.3 11.9 %collective-permute-start.8 = (bf16[16,48,256]{2,1,0:T(8,128)(2,1)S(1)}, bf16[16,48,256]{2,1,0:T(8,128)(2,1)S(1)}, u32[]{:S(2)}, u32[]{:S(2)}) collective-permute-start(bf16[16,48,256]{2,1,0:T(8,128)(2,1)S(1)} %get-tuple-element.29.refs_0_.refs_7_), channel_id=1, source_target_pairs={{0,3},{1,0},{2,1},{3,2},{4,7},{5,4},{6,5},{7,6},{8,11},{9,8},{10,9... | collective-permute-start | bytes 1179656 | tf_op jit(solution)/shard_map/ppermute | solution.py:389
  29.3 8.9 %collective-permute-start.7 = (bf16[16,48,256]{2,1,0:T(8,128)(2,1)S(1)}, bf16[16,48,256]{2,1,0:T(8,128)(2,1)S(1)}, u32[]{:S(2)}, u32[]{:S(2)}) collective-permute-start(bf16[16,48,256]{2,1,0:T(8,128)(2,1)S(1)} %get-tuple-element.29.refs_0_.refs_7_), channel_id=1, source_target_pairs={{0,2},{1,3},{2,0},{3,1},{4,6},{5,7},{6,4},{7,5},{8,10},{9,11},{10,... | collective-permute-start | bytes 1179656 | tf_op jit(solution)/shard_map/ppermute | solution.py:389
  29.7 12.2 %collective-permute-start.6 = (bf16[16,48,256]{2,1,0:T(8,128)(2,1)S(1)}, bf16[16,48,256]{2,1,0:T(8,128)(2,1)S(1)}, u32[]{:S(2)}, u32[]{:S(2)}) collective-permute-start(bf16[16,48,256]{2,1,0:T(8,128)(2,1)S(1)} %get-tuple-element.29.refs_0_.refs_7_), channel_id=1, source_target_pairs={{0,1},{1,2},{2,3},{3,0},{4,5},{5,6},{6,7},{7,4},{8,9},{9,10},{10,1... | collective-permute-start | bytes 1179656 | tf_op jit(solution)/shard_map/ppermute | solution.py:389
  30.7 22.7 %collective-permute-start.5 = (bf16[16,48,256]{2,1,0:T(8,128)(2,1)S(1)}, bf16[16,48,256]{2,1,0:T(8,128)(2,1)S(1)}, u32[]{:S(2)}, u32[]{:S(2)}) collective-permute-start(bf16[16,48,256]{2,1,0:T(8,128)(2,1)S(1)} %get-tuple-element.30.refs_0_), channel_id=1, source_target_pairs={{0,3},{1,0},{2,1},{3,2},{4,7},{5,4},{6,5},{7,6},{8,11},{9,8},{10,9... | collective-permute-start | bytes 1179656 | tf_op jit(solution)/shard_map/ppermute | solution.py:389
  33.1 20.3 %collective-permute-start.4 = (bf16[16,48,256]{2,1,0:T(8,128)(2,1)S(1)}, bf16[16,48,256]{2,1,0:T(8,128)(2,1)S(1)}, u32[]{:S(2)}, u32[]{:S(2)}) collective-permute-start(bf16[16,48,256]{2,1,0:T(8,128)(2,1)S(1)} %get-tuple-element.30.refs_0_), channel_id=1, source_target_pairs={{0,2},{1,3},{2,0},{3,1},{4,6},{5,7},{6,4},{7,5},{8,10},{9,11},{10,... | collective-permute-start | bytes 1179656 | tf_op jit(solution)/shard_map/ppermute | solution.py:389
  38.2 15.2 %collective-permute-start.3 = (bf16[16,48,256]{2,1,0:T(8,128)(2,1)S(1)}, bf16[16,48,256]{2,1,0:T(8,128)(2,1)S(1)}, u32[]{:S(2)}, u32[]{:S(2)}) collective-permute-start(bf16[16,48,256]{2,1,0:T(8,128)(2,1)S(1)} %get-tuple-element.30.refs_0_), channel_id=1, source_target_pairs={{0,1},{1,2},{2,3},{3,0},{4,5},{5,6},{6,7},{7,4},{8,9},{9,10},{10,1... | collective-permute-start | bytes 1179656 | tf_op jit(solution)/shard_map/ppermute | solution.py:389
  50.9 16.8 %collective-permute-start.12 = (bf16[16,56,256]{2,1,0:T(8,128)(2,1)S(1)}, bf16[16,56,256]{2,1,0:T(8,128)(2,1)S(1)}, u32[]{:S(2)}, u32[]{:S(2)}) collective-permute-start(bf16[16,56,256]{2,1,0:T(8,128)(2,1)S(1)} %get-tuple-element.24), channel_id=1, source_target_pairs={{0,3},{1,0},{2,1},{3,2},{4,7},{5,4},{6,5},{7,6},{8,11},{9,8},{10,9... | collective-permute-start | bytes 1376264 | tf_op jit(solution)/shard_map/ppermute | solution.py:389
  62.3 17.6 %collective-permute-start.9 = (bf16[16,56,256]{2,1,0:T(8,128)(2,1)S(1)}, bf16[16,56,256]{2,1,0:T(8,128)(2,1)S(1)}, u32[]{:S(2)}, u32[]{:S(2)}) collective-permute-start(bf16[16,56,256]{2,1,0:T(8,128)(2,1)S(1)} %get-tuple-element.21), channel_id=1, source_target_pairs={{0,3},{1,0},{2,1},{3,2},{4,7},{5,4},{6,5},{7,6},{8,11},{9,8},{10,9... | collective-permute-start | bytes 1376264 | tf_op jit(solution)/shard_map/ppermute | solution.py:389
  64.7 8.9 %collective-permute-start.13 = (bf16[16,56,256]{2,1,0:T(8,128)(2,1)S(1)}, bf16[16,56,256]{2,1,0:T(8,128)(2,1)S(1)}, u32[]{:S(2)}, u32[]{:S(2)}) collective-permute-start(bf16[16,56,256]{2,1,0:T(8,128)(2,1)S(1)} %get-tuple-element.25), channel_id=1, source_target_pairs={{0,2},{1,3},{2,0},{3,1},{4,6},{5,7},{6,4},{7,5},{8,10},{9,11},{10,... | collective-permute-start | bytes 1376264 | tf_op jit(solution)/shard_map/ppermute | solution.py:389
  64.7 13.8 %collective-permute-start.14 = (bf16[16,56,256]{2,1,0:T(8,128)(2,1)S(1)}, bf16[16,56,256]{2,1,0:T(8,128)(2,1)S(1)}, u32[]{:S(2)}, u32[]{:S(2)}) collective-permute-start(bf16[16,56,256]{2,1,0:T(8,128)(2,1)S(1)} %get-tuple-element.26), channel_id=1, source_target_pairs={{0,1},{1,2},{2,3},{3,0},{4,5},{5,6},{6,7},{7,4},{8,9},{9,10},{10,1... | collective-permute-start | bytes 1376264 | tf_op jit(solution)/shard_map/ppermute | solution.py:389
  65.4 18.1 %collective-permute-start.10 = (bf16[16,56,256]{2,1,0:T(8,128)(2,1)S(1)}, bf16[16,56,256]{2,1,0:T(8,128)(2,1)S(1)}, u32[]{:S(2)}, u32[]{:S(2)}) collective-permute-start(bf16[16,56,256]{2,1,0:T(8,128)(2,1)S(1)} %get-tuple-element.22), channel_id=1, source_target_pairs={{0,2},{1,3},{2,0},{3,1},{4,6},{5,7},{6,4},{7,5},{8,10},{9,11},{10,... | collective-permute-start | bytes 1376264 | tf_op jit(solution)/shard_map/ppermute | solution.py:389
  67.7 20.5 %collective-permute-start.11 = (bf16[16,56,256]{2,1,0:T(8,128)(2,1)S(1)}, bf16[16,56,256]{2,1,0:T(8,128)(2,1)S(1)}, u32[]{:S(2)}, u32[]{:S(2)}) collective-permute-start(bf16[16,56,256]{2,1,0:T(8,128)(2,1)S(1)} %get-tuple-element.23), channel_id=1, source_target_pairs={{0,1},{1,2},{2,3},{3,0},{4,5},{5,6},{6,7},{7,4},{8,9},{9,10},{10,1... | collective-permute-start | bytes 1376264 | tf_op jit(solution)/shard_map/ppermute | solution.py:389
  105.1 5.7 %collective-permute-start.15 = (bf16[24,512]{1,0:T(8,128)(2,1)S(1)}, bf16[24,512]{1,0:T(8,128)(2,1)S(1)}, u32[]{:S(2)}, u32[]{:S(2)}) collective-permute-start(bf16[24,512]{1,0:T(8,128)(2,1)S(1)} %get-tuple-element.28), channel_id=1, source_target_pairs={{0,16},{16,0},{1,17},{17,1},{2,18},{18,2},{3,19},{19,3},{4,20},{20... | collective-permute-start | bytes 73736 | tf_op jit(solution)/shard_map/ppermute | solution.py:380

commit v2 on v1

--- a/solution.py
+++ b/solution.py
@@ -304,7 +304,7 @@
     return numer, jnp.concatenate([tail, jnp.zeros((8, WIDE - 128), F32)], axis=1)
 
 
-def merge_kernel(p0, p1, p2, p3, after, out):
+def merge_kernel(p0, p1, p2, p3, i1, i2, i3, out, o1, o2, o3):
     spread = make_spread().astype(BF16)
     is_top = lax.broadcasted_iota(jnp.int32, (8, 128), 1) % 16 < NH
     for b in range(16):
@@ -314,14 +314,17 @@
 
 def merge(parts, after):
     vmem = pl.BlockSpec(memory_space=pltpu.VMEM)
+    whole = pl.BlockSpec(memory_space=pl.ANY)
+    block = jax.ShapeDtypeStruct((16, 56, WIDE), BF16)
     return pl.pallas_call(
         merge_kernel,
-        out_shape=jax.ShapeDtypeStruct((16, 56, WIDE), BF16),
-        in_specs=[vmem] * 4 + [pl.BlockSpec(memory_space=pl.ANY)],
-        out_specs=vmem,
+        out_shape=[block] * 4,
+        in_specs=[vmem] * 4 + [whole] * 3,
+        out_specs=[vmem] + [whole] * 3,
+        input_output_aliases={4: 1, 5: 2, 6: 3},
         compiler_params=pltpu.CompilerParams(vmem_limit_bytes=10 * 2**20),
         name="merge",
-    )(*parts, after)
+    )(*parts, *after)
 
 
 def settle_rows(got, c):
@@ -390,8 +393,7 @@
 
 
 def ring(x, axes):
-    far = shift(x, axes, 2)
-    return [x, shift(x, axes, 1), far, shift(x, axes, 3)]
+    return [x] + [shift(x, axes, by) for by in (1, 2, 3)]
 
 
 def spot(y, c, z, x):
@@ -408,8 +410,7 @@
 
 
 def deliver(parts, axes):
-    far = shift(parts[2], axes, -2)
-    return [parts[0], shift(parts[1], axes, -1), far, shift(parts[3], axes, -3)]
+    return [parts[0]] + [shift(parts[by], axes, -by) for by in (1, 2, 3)]
 
 
 def body(queries, keys, values, frame_slot, covisible, counts, out_weight):
@@ -436,8 +437,8 @@
 
     early = attend(me, need, q_parts[0], keys, k_theirs, v_turned, q_parts[0][0], 0)
     late = attend(me, need, q_parts[1], keys, k_theirs, v_turned, early[0], 1)
-    early = merge(deliver(early, "xy"), late[0])
-    keep, give = close(me, exchange(join(deliver(late, "xy"), early)))
+    early, *sent = merge(deliver(early, "xy"), late[1:])
+    keep, give = close(me, exchange(join(deliver([late[0], *sent], "xy"), early)))
     give = swap(give)
     first = core == 0
     rows = jnp.concatenate([jnp.where(first, keep, give), jnp.where(first, give, keep)], axis=1)

time: 114 us -> 109 us (0.956); the launches traced: 112 us -> 109 us
  starting transfers between devices: 30.2 us -> 28.2 us
  Pallas kernels: 26.6 us -> 24.7 us
  blocking collectives: 14.7 us -> 16.6 us
    ppermute x12, starting transfers between devices: 15.7 us -> 12.4 us  [shift(): return lax.ppermute(x, ALL, pairs)]
    pallas_call x2, Pallas kernels: 17.9 us -> 16 us  [attend(): pl.pallas_call(functools.partial(attend_kernel, part=part), out_shape=[ja...]
    all_to_all x1, blocking collectives: 14.7 us -> 16.6 us  [exchange(): return lax.all_to_all(x, ALL, 0, 0, axis_index_groups=GROUPS)]
    ppermute x4, starting transfers between devices: 6.9 us -> 8.12 us  [swap(): return lax.ppermute(x, 'core', [(0, 1), (1, 0)])]
  transfers between devices with their start and end apart: 17 -> 17, of which waited for: 10 -> 10; matrix products, arithmetic and copies ran while one was open for 2% -> 2% of each run, Pallas kernels for 22% -> 20%
where the time goes in v2:
time: 109 us
  waiting for transfers between devices  32.1 us (29%)
  starting transfers between devices  28.2 us (26%)
  Pallas kernels  24.7 us (23%)
  blocking collectives  16.6 us (15%)
  between operations  3.97 us (4%)
  local copies, waits for them, and re-layouts  1.43 us (1%)
    ppermute x12, waiting for transfers between devices, shift(): return lax.ppermute(x, ALL, pairs)  25.7 us
    all_to_all x1, blocking collectives, exchange(): return lax.all_to_all(x, ALL, 0, 0, axis_index_groups=GROUPS)  16.6 us
    pallas_call x2, Pallas kernels, attend(): pl.pallas_call(functools.partial(attend_kernel, part=part), out_shape=[ja...  16 us
    ppermute x12, starting transfers between devices, shift(): return lax.ppermute(x, ALL, pairs)  12.4 us
    ppermute x4, starting transfers between devices, swap(): return lax.ppermute(x, 'core', [(0, 1), (1, 0)])  8.12 us
    all_to_all x1, starting transfers between devices, exchange(): return lax.all_to_all(x, ALL, 0, 0, axis_index_groups=GROUPS)  7.68 us
    pallas_call x1, Pallas kernels, turn_values(): pl.pallas_call(turn_kernel, out_shape=[pltpu.HBM((8, 512, 256), BF16), ja...  3.93 us
    ppermute x4, waiting for transfers between devices, swap(): return lax.ppermute(x, 'core', [(0, 1), (1, 0)])  3.25 us
  transfers between devices with their start and end apart: 17, of which 10 were waited for; matrix products, arithmetic and copies ran while one was open for 2% of the time, Pallas kernels for 20%

profile of v2, /device:TPU:1, one launch (start us, length us, event | category | flops | bytes accessed | tf_op | source)
XLA Modules:
  0.0 108.8 jit_solution(14319941208582538588)
XLA Ops:
  0.0 1.4 %collective-permute-start.1 = (bf16[4,256,1024]{2,1,0:T(8,128)(2,1)}, bf16[4,256,1024]{2,1,0:T(8,128)(2,1)}, u32[]{:S(2)}, u32[]{:S(2)}) collective-permute-start(bf16[4,256,1024]{2,1,0:T(8,128)(2,1)} %v0.1), channel_id=1, source_target_pairs={{0,16},{16,0},{1,17},{17,1},{2,18},{18,2},{3,19},{19,3},{4,20},{20... | collective-permute-start | bytes 6291464 | tf_op jit(solution)/shard_map/ppermute | solution.py:383
  2.9 2.4 %collective-permute-done.theirs = bf16[24,512]{1,0:T(8,128)(2,1)S(1)} collective-permute-done((bf16[24,512]{1,0:T(8,128)(2,1)S(1)}, bf16[24,512]{1,0:T(8,128)(2,1)S(1)}, u32[]{:S(2)}, u32[]{:S(2)}) %collective-permute-start) | collective-permute-done | bytes 24608 | tf_op jit(solution)/shard_map/ppermute | solution.py:383
  5.3 1.5 %spread.1 = bf16[16,2,48,256]{3,2,1,0:T(8,128)(2,1)} custom-call(s32[4]{0:T(128)S(1)} %pad_add_fusion.me, bf16[24,512]{1,0:T(8,128)(2,1)S(1)} %get-tuple-element.42.mine, bf16[24,512]{1,0:T(8,128)(2,1)S(1)} %collective-permute-done.theirs), custom_call_target="tpu_custom_call" | custom-call | tf_op jit(solution)/shard_map/spread/pallas_call | solution.py:34
  6.8 7.7 %all-to-all-start = ((bf16[16,2,48,256]{3,2,1,0:T(8,128)(2,1)}), bf16[16,2,48,256]{3,2,1,0:T(8,128)(2,1)S(1)}, u32[]{:S(2)}, u32[]{:S(2)}) async-start(bf16[16,2,48,256]{3,2,1,0:T(8,128)(2,1)} %spread.1), calls=%async_computation | async-start | bytes 1572864 | tf_op jit(solution)/shard_map/all_to_all | solution.py:409
  14.6 3.9 %turn.1 = (bf16[8,512,256]{2,1,0:T(8,128)(2,1)}, s32[2]{0:T(128)S(1)}) custom-call(s32[4]{0:T(128)S(1)} %pad_add_fusion.me, bf16[4,256,1024]{2,1,0:T(8,128)(2,1)} %v0.1, bf16[4,256,1024]{2,1,0:T(8,128)(2,1)} %collective-permute-done.1.v1, bf16[4,256,1024]{2,1,0:T(8,128)(2,1)} %collective-permute-done.2.k.refs_5_), custom_call_target="tpu_custom_call" | custom-call | flops 1000000 | bytes 8388608 | tf_op jit(solution)/shard_map/turn/pallas_call | solution.py:258
  23.0 3.2 %all-to-all-done = bf16[16,2,48,256]{3,2,1,0:T(8,128)(2,1)S(1)} async-done(((bf16[16,2,48,256]{3,2,1,0:T(8,128)(2,1)}), bf16[16,2,48,256]{3,2,1,0:T(8,128)(2,1)S(1)}, u32[]{:S(2)}, u32[]{:S(2)}) %all-to-all-start) | async-done | bytes 786464 | tf_op jit(solution)/shard_map/all_to_all | solution.py:409
  26.3 3.0 %collective-permute-start.8 = (bf16[16,48,256]{2,1,0:T(8,128)(2,1)S(1)}, bf16[16,48,256]{2,1,0:T(8,128)(2,1)S(1)}, u32[]{:S(2)}, u32[]{:S(2)}) collective-permute-start(bf16[16,48,256]{2,1,0:T(8,128)(2,1)S(1)} %get-tuple-element.37.refs_0_.refs_7_), channel_id=1, source_target_pairs={{0,3},{1,0},{2,1},{3,2},{4,7},{5,4},{6,5},{7,6},{8,11},{9,8},{10,9... | collective-permute-start | bytes 1179656 | tf_op jit(solution)/shard_map/ppermute | solution.py:392
  30.7 2.4 %collective-permute-start.5 = (bf16[16,48,256]{2,1,0:T(8,128)(2,1)S(1)}, bf16[16,48,256]{2,1,0:T(8,128)(2,1)S(1)}, u32[]{:S(2)}, u32[]{:S(2)}) collective-permute-start(bf16[16,48,256]{2,1,0:T(8,128)(2,1)S(1)} %get-tuple-element.38.refs_0_), channel_id=1, source_target_pairs={{0,3},{1,0},{2,1},{3,2},{4,7},{5,4},{6,5},{7,6},{8,11},{9,8},{10,9... | collective-permute-start | bytes 1179656 | tf_op jit(solution)/shard_map/ppermute | solution.py:392
  33.1 1.3 %collective-permute-start.4 = (bf16[16,48,256]{2,1,0:T(8,128)(2,1)S(1)}, bf16[16,48,256]{2,1,0:T(8,128)(2,1)S(1)}, u32[]{:S(2)}, u32[]{:S(2)}) collective-permute-start(bf16[16,48,256]{2,1,0:T(8,128)(2,1)S(1)} %get-tuple-element.38.refs_0_), channel_id=1, source_target_pairs={{0,2},{1,3},{2,0},{3,1},{4,6},{5,7},{6,4},{7,5},{8,10},{9,11},{10,... | collective-permute-start | bytes 1179656 | tf_op jit(solution)/shard_map/ppermute | solution.py:392
  34.4 3.8 %collective-permute-done.8.refs_3_ = bf16[16,48,256]{2,1,0:T(8,128)(2,1)S(1)} collective-permute-done((bf16[16,48,256]{2,1,0:T(8,128)(2,1)S(1)}, bf16[16,48,256]{2,1,0:T(8,128)(2,1)S(1)}, u32[]{:S(2)}, u32[]{:S(2)}) %collective-permute-start.8) | collective-permute-done | bytes 393248 | tf_op jit(solution)/shard_map/ppermute | solution.py:392
  38.2 3.7 %collective-permute-done.6.refs_1_ = bf16[16,48,256]{2,1,0:T(8,128)(2,1)S(1)} collective-permute-done((bf16[16,48,256]{2,1,0:T(8,128)(2,1)S(1)}, bf16[16,48,256]{2,1,0:T(8,128)(2,1)S(1)}, u32[]{:S(2)}, u32[]{:S(2)}) %collective-permute-start.6) | collective-permute-done | bytes 393248 | tf_op jit(solution)/shard_map/ppermute | solution.py:392
  41.9 7.9 %attend.2 = (bf16[16,56,256]{2,1,0:T(8,128)(2,1)S(1)}, bf16[16,56,256]{2,1,0:T(8,128)(2,1)S(1)}, bf16[16,56,256]{2,1,0:T(8,128)(2,1)S(1)}, bf16[16,56,256]{2,1,0:T(8,128)(2,1)S(1)}) custom-call(s32[4]{0:T(128)S(1)} %pad_add_fusion.me, s32[12,8]{1,0:T(8,128)S(1)} %convert_element_type.6.need, bf16[16,48,256]{2,1,0:T(8,128)(2,1)S(1)} %get-tuple-element.37.refs_0_.refs_7_, ...), custom_call_target="tpu_custom_call" | custom-call | flops 10000000000 | bytes 8388608 | tf_op jit(solution)/shard_map/attend/pallas_call | solution.py:207
  49.8 2.7 %collective-permute-start.9 = (bf16[16,56,256]{2,1,0:T(8,128)(2,1)S(1)}, bf16[16,56,256]{2,1,0:T(8,128)(2,1)S(1)}, u32[]{:S(2)}, u32[]{:S(2)}) collective-permute-start(bf16[16,56,256]{2,1,0:T(8,128)(2,1)S(1)} %get-tuple-element.25), channel_id=1, source_target_pairs={{0,3},{1,0},{2,1},{3,2},{4,7},{5,4},{6,5},{7,6},{8,11},{9,8},{10,9... | collective-permute-start | bytes 1376264 | tf_op jit(solution)/shard_map/ppermute | solution.py:392
  53.2 8.1 %attend.3 = (bf16[16,56,256]{2,1,0:T(8,128)(2,1)S(1)}, bf16[16,56,256]{2,1,0:T(8,128)(2,1)S(1)}, bf16[16,56,256]{2,1,0:T(8,128)(2,1)S(1)}, bf16[16,56,256]{2,1,0:T(8,128)(2,1)S(1)}) custom-call(s32[4]{0:T(128)S(1)} %pad_add_fusion.me, s32[12,8]{1,0:T(8,128)S(1)} %convert_element_type.6.need, bf16[16,48,256]{2,1,0:T(8,128)(2,1)S(1)} %get-tuple-element.38.refs_0_, ...), custom_call_target="tpu_custom_call" | custom-call | flops 10000000000 | bytes 8388608 | tf_op jit(solution)/shard_map/attend/pallas_call | solution.py:207
  61.3 1.6 %collective-permute-done.9.p1 = bf16[16,56,256]{2,1,0:T(8,128)(2,1)S(1)} collective-permute-done((bf16[16,56,256]{2,1,0:T(8,128)(2,1)S(1)}, bf16[16,56,256]{2,1,0:T(8,128)(2,1)S(1)}, u32[]{:S(2)}, u32[]{:S(2)}) %collective-permute-start.9) | collective-permute-done | bytes 458784 | tf_op jit(solution)/shard_map/ppermute | solution.py:392
  62.8 3.7 %collective-permute-done.11.p3 = bf16[16,56,256]{2,1,0:T(8,128)(2,1)S(1)} collective-permute-done((bf16[16,56,256]{2,1,0:T(8,128)(2,1)S(1)}, bf16[16,56,256]{2,1,0:T(8,128)(2,1)S(1)}, u32[]{:S(2)}, u32[]{:S(2)}) %collective-permute-start.11) | collective-permute-done | bytes 458784 | tf_op jit(solution)/shard_map/ppermute | solution.py:392
  66.5 1.1 merge.1
  69.2 6.2 %collective-permute-done.12.p1 = bf16[16,56,256]{2,1,0:T(8,128)(2,1)S(1)} collective-permute-done((bf16[16,56,256]{2,1,0:T(8,128)(2,1)S(1)}, bf16[16,56,256]{2,1,0:T(8,128)(2,1)S(1)}, u32[]{:S(2)}, u32[]{:S(2)}) %collective-permute-start.12) | collective-permute-done | bytes 458784 | tf_op jit(solution)/shard_map/ppermute | solution.py:392
  75.3 1.9 %collective-permute-done.13.p2 = bf16[16,56,256]{2,1,0:T(8,128)(2,1)S(1)} collective-permute-done((bf16[16,56,256]{2,1,0:T(8,128)(2,1)S(1)}, bf16[16,56,256]{2,1,0:T(8,128)(2,1)S(1)}, u32[]{:S(2)}, u32[]{:S(2)}) %collective-permute-start.13) | collective-permute-done | bytes 458784 | tf_op jit(solution)/shard_map/ppermute | solution.py:392
  77.2 4.9 %collective-permute-done.14.p3 = bf16[16,56,256]{2,1,0:T(8,128)(2,1)S(1)} collective-permute-done((bf16[16,56,256]{2,1,0:T(8,128)(2,1)S(1)}, bf16[16,56,256]{2,1,0:T(8,128)(2,1)S(1)}, u32[]{:S(2)}, u32[]{:S(2)}) %collective-permute-start.14) | collective-permute-done | bytes 458784 | tf_op jit(solution)/shard_map/ppermute | solution.py:392
  82.1 1.1 join.1
  83.1 16.6 %all_to_all.10.got = bf16[16,2,56,256]{3,2,1,0:T(8,128)(2,1)S(1)} all-to-all(bf16[16,2,56,256]{3,2,1,0:T(8,128)(2,1)S(1)} %join.1), channel_id=1, replica_groups={{0,32,64,96,4,36,68,100,8,40,72,104,12,44,76,108},{1,33,65,97,5,37,69,1..., dimensions={0} | all-to-all | bytes 1835008 | tf_op jit(solution)/shard_map/all_to_all | solution.py:409
  99.7 1.1 %close.1 = (bf16[24,512]{1,0:T(8,128)(2,1)S(1)}, bf16[24,512]{1,0:T(8,128)(2,1)S(1)}) custom-call(s32[4]{0:T(128)S(1)} %pad_add_fusion.me, bf16[16,2,56,256]{3,2,1,0:T(8,128)(2,1)S(1)} %all_to_all.10.got), custom_call_target="tpu_custom_call" | custom-call | tf_op jit(solution)/shard_map/close/pallas_call | solution.py:371
  100.8 6.1 %collective-permute-start.15 = (bf16[24,512]{1,0:T(8,128)(2,1)S(1)}, bf16[24,512]{1,0:T(8,128)(2,1)S(1)}, u32[]{:S(2)}, u32[]{:S(2)}) collective-permute-start(bf16[24,512]{1,0:T(8,128)(2,1)S(1)} %get-tuple-element.36), channel_id=1, source_target_pairs={{0,16},{16,0},{1,17},{17,1},{2,18},{18,2},{3,19},{19,3},{4,20},{20... | collective-permute-start | bytes 73736 | tf_op jit(solution)/shard_map/ppermute | solution.py:383
  (38 shorter events, 7.7 us)
Async XLA Ops:
  0.0 107.8 %copy-start = (bf16[1024,1024]{1,0:T(8,128)(2,1)S(1)}, bf16[1024,1024]{1,0:T(8,128)(2,1)}, u32[]{:S(2)}) copy-start(bf16[1024,1024]{1,0:T(8,128)(2,1)} %param.13) | copy-start | bytes 6291460
  0.0 14.6 %collective-permute-start.1 = (bf16[4,256,1024]{2,1,0:T(8,128)(2,1)}, bf16[4,256,1024]{2,1,0:T(8,128)(2,1)}, u32[]{:S(2)}, u32[]{:S(2)}) collective-permute-start(bf16[4,256,1024]{2,1,0:T(8,128)(2,1)} %v0.1), channel_id=1, source_target_pairs={{0,16},{16,0},{1,17},{17,1},{2,18},{18,2},{3,19},{19,3},{4,20},{20... | collective-permute-start | bytes 6291464 | tf_op jit(solution)/shard_map/ppermute | solution.py:383
  1.4 13.2 %collective-permute-start.2 = (bf16[4,256,1024]{2,1,0:T(8,128)(2,1)}, bf16[4,256,1024]{2,1,0:T(8,128)(2,1)}, u32[]{:S(2)}, u32[]{:S(2)}) collective-permute-start(bf16[4,256,1024]{2,1,0:T(8,128)(2,1)} %refs_4_.3), channel_id=1, source_target_pairs={{0,16},{16,0},{1,17},{17,1},{2,18},{18,2},{3,19},{19,3},{4,20},{20... | collective-permute-start | bytes 6291464 | tf_op jit(solution)/shard_map/ppermute | solution.py:383
  2.2 3.1 %collective-permute-start = (bf16[24,512]{1,0:T(8,128)(2,1)S(1)}, bf16[24,512]{1,0:T(8,128)(2,1)S(1)}, u32[]{:S(2)}, u32[]{:S(2)}) collective-permute-start(bf16[24,512]{1,0:T(8,128)(2,1)S(1)} %get-tuple-element.41), channel_id=1, source_target_pairs={{0,16},{16,0},{1,17},{17,1},{2,18},{18,2},{3,19},{19,3},{4,20},{20... | collective-permute-start | bytes 73736 | tf_op jit(solution)/shard_map/ppermute | solution.py:383
  6.8 19.4 %all-to-all-start = ((bf16[16,2,48,256]{3,2,1,0:T(8,128)(2,1)}), bf16[16,2,48,256]{3,2,1,0:T(8,128)(2,1)S(1)}, u32[]{:S(2)}, u32[]{:S(2)}) async-start(bf16[16,2,48,256]{3,2,1,0:T(8,128)(2,1)} %spread.1), calls=%async_computation | async-start | bytes 1572864 | tf_op jit(solution)/shard_map/all_to_all | solution.py:409
  14.6 15.4 %copy-start.2 = (s32[512]{0:T(512)S(1)}, s32[512]{0:T(512)}, u32[]{:S(2)}) copy-start(s32[512]{0:T(512)} %param.10) | copy-start | bytes 6148
  14.6 15.6 %copy-start.3 = (s32[12]{0:T(128)S(1)}, s32[12]{0:T(128)}, u32[]{:S(2)}) copy-start(s32[12]{0:T(128)} %param.12) | copy-start | bytes 148
  14.6 15.7 %copy-start.1 = (s32[12,160]{1,0:T(8,128)S(1)}, s32[12,160]{1,0:T(8,128)}, u32[]{:S(2)}) copy-start(s32[12,160]{1,0:T(8,128)} %param.11) | copy-start | bytes 23044
  26.3 11.9 %collective-permute-start.8 = (bf16[16,48,256]{2,1,0:T(8,128)(2,1)S(1)}, bf16[16,48,256]{2,1,0:T(8,128)(2,1)S(1)}, u32[]{:S(2)}, u32[]{:S(2)}) collective-permute-start(bf16[16,48,256]{2,1,0:T(8,128)(2,1)S(1)} %get-tuple-element.37.refs_0_.refs_7_), channel_id=1, source_target_pairs={{0,3},{1,0},{2,1},{3,2},{4,7},{5,4},{6,5},{7,6},{8,11},{9,8},{10,9... | collective-permute-start | bytes 1179656 | tf_op jit(solution)/shard_map/ppermute | solution.py:392
  29.3 8.9 %collective-permute-start.7 = (bf16[16,48,256]{2,1,0:T(8,128)(2,1)S(1)}, bf16[16,48,256]{2,1,0:T(8,128)(2,1)S(1)}, u32[]{:S(2)}, u32[]{:S(2)}) collective-permute-start(bf16[16,48,256]{2,1,0:T(8,128)(2,1)S(1)} %get-tuple-element.37.refs_0_.refs_7_), channel_id=1, source_target_pairs={{0,2},{1,3},{2,0},{3,1},{4,6},{5,7},{6,4},{7,5},{8,10},{9,11},{10,... | collective-permute-start | bytes 1179656 | tf_op jit(solution)/shard_map/ppermute | solution.py:392
  29.7 12.2 %collective-permute-start.6 = (bf16[16,48,256]{2,1,0:T(8,128)(2,1)S(1)}, bf16[16,48,256]{2,1,0:T(8,128)(2,1)S(1)}, u32[]{:S(2)}, u32[]{:S(2)}) collective-permute-start(bf16[16,48,256]{2,1,0:T(8,128)(2,1)S(1)} %get-tuple-element.37.refs_0_.refs_7_), channel_id=1, source_target_pairs={{0,1},{1,2},{2,3},{3,0},{4,5},{5,6},{6,7},{7,4},{8,9},{9,10},{10,1... | collective-permute-start | bytes 1179656 | tf_op jit(solution)/shard_map/ppermute | solution.py:392
  30.7 22.3 %collective-permute-start.5 = (bf16[16,48,256]{2,1,0:T(8,128)(2,1)S(1)}, bf16[16,48,256]{2,1,0:T(8,128)(2,1)S(1)}, u32[]{:S(2)}, u32[]{:S(2)}) collective-permute-start(bf16[16,48,256]{2,1,0:T(8,128)(2,1)S(1)} %get-tuple-element.38.refs_0_), channel_id=1, source_target_pairs={{0,3},{1,0},{2,1},{3,2},{4,7},{5,4},{6,5},{7,6},{8,11},{9,8},{10,9... | collective-permute-start | bytes 1179656 | tf_op jit(solution)/shard_map/ppermute | solution.py:392
  33.1 20.1 %collective-permute-start.4 = (bf16[16,48,256]{2,1,0:T(8,128)(2,1)S(1)}, bf16[16,48,256]{2,1,0:T(8,128)(2,1)S(1)}, u32[]{:S(2)}, u32[]{:S(2)}) collective-permute-start(bf16[16,48,256]{2,1,0:T(8,128)(2,1)S(1)} %get-tuple-element.38.refs_0_), channel_id=1, source_target_pairs={{0,2},{1,3},{2,0},{3,1},{4,6},{5,7},{6,4},{7,5},{8,10},{9,11},{10,... | collective-permute-start | bytes 1179656 | tf_op jit(solution)/shard_map/ppermute | solution.py:392
  38.2 15.0 %collective-permute-start.3 = (bf16[16,48,256]{2,1,0:T(8,128)(2,1)S(1)}, bf16[16,48,256]{2,1,0:T(8,128)(2,1)S(1)}, u32[]{:S(2)}, u32[]{:S(2)}) collective-permute-start(bf16[16,48,256]{2,1,0:T(8,128)(2,1)S(1)} %get-tuple-element.38.refs_0_), channel_id=1, source_target_pairs={{0,1},{1,2},{2,3},{3,0},{4,5},{5,6},{6,7},{7,4},{8,9},{9,10},{10,1... | collective-permute-start | bytes 1179656 | tf_op jit(solution)/shard_map/ppermute | solution.py:392
  49.8 13.0 %collective-permute-start.9 = (bf16[16,56,256]{2,1,0:T(8,128)(2,1)S(1)}, bf16[16,56,256]{2,1,0:T(8,128)(2,1)S(1)}, u32[]{:S(2)}, u32[]{:S(2)}) collective-permute-start(bf16[16,56,256]{2,1,0:T(8,128)(2,1)S(1)} %get-tuple-element.25), channel_id=1, source_target_pairs={{0,3},{1,0},{2,1},{3,2},{4,7},{5,4},{6,5},{7,6},{8,11},{9,8},{10,9... | collective-permute-start | bytes 1376264 | tf_op jit(solution)/shard_map/ppermute | solution.py:392
  52.5 10.3 %collective-permute-start.10 = (bf16[16,56,256]{2,1,0:T(8,128)(2,1)S(1)}, bf16[16,56,256]{2,1,0:T(8,128)(2,1)S(1)}, u32[]{:S(2)}, u32[]{:S(2)}) collective-permute-start(bf16[16,56,256]{2,1,0:T(8,128)(2,1)S(1)} %get-tuple-element.26), channel_id=1, source_target_pairs={{0,2},{1,3},{2,0},{3,1},{4,6},{5,7},{6,4},{7,5},{8,10},{9,11},{10,... | collective-permute-start | bytes 1376264 | tf_op jit(solution)/shard_map/ppermute | solution.py:392
  52.9 13.6 %collective-permute-start.11 = (bf16[16,56,256]{2,1,0:T(8,128)(2,1)S(1)}, bf16[16,56,256]{2,1,0:T(8,128)(2,1)S(1)}, u32[]{:S(2)}, u32[]{:S(2)}) collective-permute-start(bf16[16,56,256]{2,1,0:T(8,128)(2,1)S(1)} %get-tuple-element.27), channel_id=1, source_target_pairs={{0,1},{1,2},{2,3},{3,0},{4,5},{5,6},{6,7},{7,4},{8,9},{9,10},{10,1... | collective-permute-start | bytes 1376264 | tf_op jit(solution)/shard_map/ppermute | solution.py:392
  67.6 7.7 %collective-permute-start.12 = (bf16[16,56,256]{2,1,0:T(8,128)(2,1)S(1)}, bf16[16,56,256]{2,1,0:T(8,128)(2,1)S(1)}, u32[]{:S(2)}, u32[]{:S(2)}) collective-permute-start(bf16[16,56,256]{2,1,0:T(8,128)(2,1)S(1)} %get-tuple-element.31), channel_id=1, source_target_pairs={{0,3},{1,0},{2,1},{3,2},{4,7},{5,4},{6,5},{7,6},{8,11},{9,8},{10,9... | collective-permute-start | bytes 1376264 | tf_op jit(solution)/shard_map/ppermute | solution.py:392
  68.0 9.2 %collective-permute-start.13 = (bf16[16,56,256]{2,1,0:T(8,128)(2,1)S(1)}, bf16[16,56,256]{2,1,0:T(8,128)(2,1)S(1)}, u32[]{:S(2)}, u32[]{:S(2)}) collective-permute-start(bf16[16,56,256]{2,1,0:T(8,128)(2,1)S(1)} %get-tuple-element.32), channel_id=1, source_target_pairs={{0,2},{1,3},{2,0},{3,1},{4,6},{5,7},{6,4},{7,5},{8,10},{9,11},{10,... | collective-permute-start | bytes 1376264 | tf_op jit(solution)/shard_map/ppermute | solution.py:392
  68.5 13.6 %collective-permute-start.14 = (bf16[16,56,256]{2,1,0:T(8,128)(2,1)S(1)}, bf16[16,56,256]{2,1,0:T(8,128)(2,1)S(1)}, u32[]{:S(2)}, u32[]{:S(2)}) collective-permute-start(bf16[16,56,256]{2,1,0:T(8,128)(2,1)S(1)} %get-tuple-element.33), channel_id=1, source_target_pairs={{0,1},{1,2},{2,3},{3,0},{4,5},{5,6},{6,7},{7,4},{8,9},{9,10},{10,1... | collective-permute-start | bytes 1376264 | tf_op jit(solution)/shard_map/ppermute | solution.py:392
  100.8 6.9 %collective-permute-start.15 = (bf16[24,512]{1,0:T(8,128)(2,1)S(1)}, bf16[24,512]{1,0:T(8,128)(2,1)S(1)}, u32[]{:S(2)}, u32[]{:S(2)}) collective-permute-start(bf16[24,512]{1,0:T(8,128)(2,1)S(1)} %get-tuple-element.36), channel_id=1, source_target_pairs={{0,16},{16,0},{1,17},{17,1},{2,18},{18,2},{3,19},{19,3},{4,20},{20... | collective-permute-start | bytes 73736 | tf_op jit(solution)/shard_map/ppermute | solution.py:383
